TPU v7x, 32 devices: a whole 2x2x4 slice. The times are simulated.
32 devices in a mesh: freq: 4 (over y, core), tri: 8 (over z, x).
Axes of the slice: x: 2, y: 2, z: 4, core: 2. Of those that a mesh axis runs over, the one named last changes fastest.
Arguments:
- voltages: int32 [2, 8, 256, 66304], P(None, 'tri', 'freq'), may hold values from -8 to 7
- window_taps: float32 [4, 256], replicated, may hold values from -3 to 3
Outputs:
- visibility: bfloat16 [128, 8, 5, 256, 2, 256], P('freq', 'tri')
All inputs are finite; a program needn't handle non-finite values.
Results may differ from a plain program's by a relative error of at most 0.0055.
Values may be sent and summed in bfloat16 or wider, within the bound.
No kernel may reach another device: no remote copies, remote signals or barrier semaphores. Data moves between devices by JAX's collectives and lax.ppermute only.
A program may use at most 384 MiB of HBM per device.

v0:
```python
import math

import jax
import jax.numpy as jnp
from jax import lax
from jax.sharding import PartitionSpec as P

CHAN = 128


spectrum_scale = 1.0 / 128.0


def passed_along(value, axis, steps):
    count = lax.axis_size(axis)
    pairs = [(source, (source + steps) % count) for source in range(count)]
    return lax.ppermute(value, axis, pairs)


def fourier_table(points, chans):
    point_index = jnp.arange(points, dtype=jnp.int32)[:, None]
    chan_index = jnp.arange(chans, dtype=jnp.int32)[None, :]
    phase = (point_index * chan_index % points).astype(jnp.float32) * (2.0 * math.pi / points)
    cosine = jnp.cos(phase)
    sine = jnp.sin(phase)
    table = jnp.stack([jnp.stack([cosine, -sine], -1), jnp.stack([sine, cosine], -1)], 0)
    return table * spectrum_scale


def fir_frames(samples, window_taps, count):
    frames = samples[:, :, 0:count, :] * window_taps[0]
    for tap_index in range(1, window_taps.shape[0]):
        frames = frames + samples[:, :, tap_index : tap_index + count, :] * window_taps[tap_index]
    return frames


def cross_tile(left_rows, right_block):
    spectra_len = right_block.shape[-1]
    real_part = right_block[..., 0, :]
    imag_part = right_block[..., 1, :]
    stacked = jnp.stack(
        [jnp.concatenate([real_part, imag_part], -1), jnp.concatenate([-imag_part, real_part], -1)],
        axis=-3,
    )
    product = jnp.einsum(
        "...at,...nbt->...anb", left_rows, stacked, preferred_element_type=jnp.float32
    )
    return (product * (1.0 / spectra_len)).astype(jnp.bfloat16)


def on_device(voltages, window_taps):
    taps_count, points = window_taps.shape
    in_dev = voltages.shape[2]
    frames_total = voltages.shape[3] // points
    spectra_len = frames_total - taps_count + 1
    samples = voltages.reshape(2, in_dev, frames_total, points).astype(jnp.float32)
    frames = fir_frames(samples, window_taps, spectra_len)
    spectra = jnp.einsum(
        "qpcr,qimp->cirm", fourier_table(points, CHAN), frames, precision=lax.Precision.HIGHEST
    ).astype(jnp.bfloat16)
    blocks = lax.axis_size("tri")
    half_count = blocks // 2
    own_block = lax.all_to_all(spectra, "freq", split_axis=0, concat_axis=1, tiled=True)
    group_chans = own_block.shape[0]
    block_len = own_block.shape[1]
    left_rows = own_block.reshape(group_chans, block_len, 2 * spectra_len)
    held = own_block[None]
    while held.shape[0] < half_count + 1:
        run_len = held.shape[0]
        count = min(run_len, half_count + 1 - run_len)
        received = passed_along(held[:count], "tri", -run_len)
        held = jnp.concatenate([held, received], 0)

    def fetch_block(offset):
        return held[offset]

    tile_list = [cross_tile(left_rows, own_block)]
    for offset in range(1, half_count):
        tile_list.append(cross_tile(left_rows, fetch_block(offset)))
    far_block = fetch_block(half_count)
    full_tile = cross_tile(left_rows, far_block)
    tile_list.append(full_tile)
    return jnp.stack(tile_list, axis=1)[:, None]


def solution(mesh):
    placed = (P(None, "tri", "freq", None), P())
    return jax.shard_map(
        on_device,
        mesh=mesh,
        in_specs=placed,
        out_specs=P("freq", "tri", None, None, None, None),
        check_vma=False,
    )
```

profile of v0, /device:TPU:26, one launch (start us, length us, event | category | flops | bytes accessed | tf_op | source)
XLA Modules:
  0.0 1358.4 jit_solution(1778706611489659910)
XLA Ops:
  1.0 22.6 %convert_element_type.51 = f32[2,1,64,66304]{3,2,1,0:T(8,128)} convert(s32[2,1,64,66304]{3,2,1,0:T(8,128)} %param.2) | non-fusion elementwise | flops 8486912 | bytes 67895296 | tf_op jit(solution)/shard_map/convert_element_type | solution.py:56
  23.6 28.8 %convert_element_type.52 = f32[2,64,259,256]{3,2,1,0:T(8,128)} reshape(f32[2,1,64,66304]{3,2,1,0:T(8,128)} %convert_element_type.51) | data formatting | bytes 67895296 | tf_op jit(solution)/shard_map/convert_element_type | solution.py:56
  52.4 69.3 %fusion.37 = bf16[128,64,2,256]{0,3,2,1:T(8,128)(2,1)} fusion(f32[1,256,128,2]{2,1,0,3:T(8,128)S(1)} %get-tuple-element.28, f32[1,256,128,2]{2,1,0,3:T(8,128)S(1)} %get-tuple-element.27, f32[2,64,259,256]{3,2,1,0:T(8,128)} %convert_element_type.52, f32[256]{0:T(256)S(1)} %bitcast.144, f32[256]{0:T(256)S(1)} %bitcast.145, f32[256]{0:T(256)S(1)} %bitcast.143, ...), kind=kOutput, calls=%fused_computation.56 | convolution fusion | flops 25832980480 | bytes 143134720 | tf_op jit(solution)/shard_map/qpcr,qimp->cirm/dot_general | solution.py:58
  121.8 21.1 %copy.31 = bf16[128,64,2,256]{3,2,1,0:T(2,128)(2,1)} copy(bf16[128,64,2,256]{0,3,2,1:T(8,128)(2,1)} %fusion.37) | data formatting | bytes 16777216 | tf_op jit(solution)/shard_map/convert_element_type | solution.py:60
  142.8 100.6 %all_to_all.18 = bf16[128,64,2,256]{3,2,1,0:T(2,128)(2,1)} all-to-all(bf16[128,64,2,256]{3,2,1,0:T(2,128)(2,1)} %copy.31), channel_id=1, replica_groups=mesh['freq'=4,'tri'=8] {'freq'}, dimensions={0} | all-to-all | bytes 16777216 | tf_op jit(solution)/shard_map/all_to_all | solution.py:63
  243.4 8.6 copy.32
  251.9 8.3 copy.34
  260.8 184.2 %collective-permute-done = bf16[1,32,256,2,256]{4,2,1,3,0:T(8,128)(2,1)S(1)} collective-permute-done((bf16[1,32,256,2,256]{4,2,1,3,0:T(8,128)(2,1)}, bf16[1,32,256,2,256]{4,2,1,3,0:T(8,128)(2,1)S(1)}, u32[]{:S(2)}, u32[]{:S(2)}) %collective-permute-start) | collective-permute-done | bytes 8388640 | tf_op jit(solution)/shard_map/ppermute | solution.py:17
  445.0 12.2 pad_maximum_fusion
  457.3 8.1 copy.33
  465.4 14.0 %reshape.93 = bf16[32,256,512,1]{2,1,0,3:T(8,128)(2,1)} reshape(bf16[32,4,64,2,256]{4,3,2,1,0:T(2,128)(2,1)} %copy.33) | data formatting | bytes 16777216 | tf_op jit(solution)/shard_map/reshape | solution.py:66
  485.7 6.2 maximum_bitcast_fusion
  491.9 13.1 bitcast_dynamic-update-slice_fusion.4
  507.6 671.1 %collective-permute-done.2 = bf16[1,32,256,2,256]{4,2,1,3,0:T(8,128)(2,1)} collective-permute-done((bf16[1,32,256,2,256]{4,2,1,3,0:T(8,128)(2,1)}, bf16[1,32,256,2,256]{4,2,1,3,0:T(8,128)(2,1)}, u32[]{:S(2)}, u32[]{:S(2)}) %collective-permute-start.2) | collective-permute-done | bytes 8388640 | tf_op jit(solution)/shard_map/ppermute | solution.py:17
  1185.9 6.1 maximum_bitcast_fusion.2
  1192.1 6.1 maximum_bitcast_fusion.8
  1198.2 13.0 bitcast_dynamic-update-slice_fusion.3
  1211.1 6.7 slice_bitcast_fusion
  1224.8 6.2 maximum_bitcast_fusion.4
  1231.1 13.1 bitcast_dynamic-update-slice_fusion.2
  1244.1 13.3 maximum_bitcast_fusion.6
  1257.4 13.2 bitcast_dynamic-update-slice_fusion.1
  1270.7 13.0 bitcast_dynamic-update-slice_fusion
  1283.7 74.7 %copy.41 = bf16[32,1,5,256,2,256]{5,4,3,2,1,0:T(2,128)(2,1)} copy(bf16[32,1,5,256,2,256]{5,3,4,0,2,1:T(8,128)(2,1)} %bitcast.141) | data formatting | bytes 83886080 | tf_op jit(solution)/shard_map/broadcast_in_dim | solution.py:83
  (32 shorter events, 24.8 us)
Async XLA Ops:
  23.6 28.8 %copy-start.1 = (f32[4,256]{1,0:T(4,128)S(1)}, f32[4,256]{1,0:T(4,128)}, u32[]{:S(2)}) copy-start(f32[4,256]{1,0:T(4,128)} %param.3) | copy-start | bytes 12292
  260.2 197.0 %slice-start = ((s8[8388608]{0:T(1024)(128)(4,1)}), s8[4194304]{0:T(1024)(128)(4,1)S(1)}, s32[]{:S(2)}) async-start(s8[8388608]{0:T(1024)(128)(4,1)} %bitcast.134), calls=%async_computation.1 | async-start | bytes 8388608
  260.2 197.0 %slice-start.1 = ((s8[8388608]{0:T(1024)(128)(4,1)}), s8[4194304]{0:T(1024)(128)(4,1)S(1)}, s32[]{:S(2)}) async-start(s8[8388608]{0:T(1024)(128)(4,1)} %bitcast.134), calls=%async_computation.2 | async-start | bytes 8388608
  260.2 184.7 %collective-permute-start = (bf16[1,32,256,2,256]{4,2,1,3,0:T(8,128)(2,1)}, bf16[1,32,256,2,256]{4,2,1,3,0:T(8,128)(2,1)S(1)}, u32[]{:S(2)}, u32[]{:S(2)}) collective-permute-start(bf16[1,32,256,2,256]{4,2,1,3,0:T(8,128)(2,1)} %bitcast.23), channel_id=1, source_target_pairs={{0,7},{1,0},{2,1},{3,2},{4,3},{5,4},{6,5},{7,6},{8,15},{9,8},{10,9... | collective-permute-start | bytes 25165832 | tf_op jit(solution)/shard_map/ppermute | solution.py:17
  445.0 12.2 copy-start
  457.2 754.0 %collective-permute-start.1 = (bf16[2,32,256,2,256]{4,2,1,3,0:T(8,128)(2,1)}, bf16[2,32,256,2,256]{4,2,1,3,0:T(8,128)(2,1)}, u32[]{:S(2)}, u32[]{:S(2)}) collective-permute-start(bf16[2,32,256,2,256]{4,2,1,3,0:T(8,128)(2,1)} %pad_maximum_fusion), channel_id=1, source_target_pairs={{0,6},{1,7},{2,0},{3,1},{4,2},{5,3},{6,4},{7,5},{8,14},{9,15},{10,... | collective-permute-start | bytes 50331656 | tf_op jit(solution)/shard_map/ppermute | solution.py:17
  457.2 721.5 %collective-permute-start.2 = (bf16[1,32,256,2,256]{4,2,1,3,0:T(8,128)(2,1)}, bf16[1,32,256,2,256]{4,2,1,3,0:T(8,128)(2,1)}, u32[]{:S(2)}, u32[]{:S(2)}) collective-permute-start(bf16[1,32,256,2,256]{4,2,1,3,0:T(8,128)(2,1)} %bitcast.23), channel_id=1, source_target_pairs={{0,4},{1,5},{2,6},{3,7},{4,0},{5,1},{6,2},{7,3},{8,12},{9,13},{10,... | collective-permute-start | bytes 25165832 | tf_op jit(solution)/shard_map/ppermute | solution.py:17
  505.0 676.2 %slice-start.2 = ((s8[8388608]{0:T(1024)(128)(4,1)}), s8[4194304]{0:T(1024)(128)(4,1)S(1)}, s32[]{:S(2)}) async-start(s8[8388608]{0:T(1024)(128)(4,1)} %bitcast.138), calls=%async_computation.3 | async-start | bytes 8388608
  507.6 673.6 %slice-start.3 = ((s8[8388608]{0:T(1024)(128)(4,1)}), s8[4194304]{0:T(1024)(128)(4,1)S(1)}, s32[]{:S(2)}) async-start(s8[8388608]{0:T(1024)(128)(4,1)} %bitcast.138), calls=%async_computation.4 | async-start | bytes 8388608
where the time goes:
time: 1360 us
  waiting for transfers between devices  855 us (63%)
  local copies, waits for them, and re-layouts  183 us (13%)
  matrix products  135 us (10%)
  blocking collectives  101 us (7%)
  other arithmetic  83.9 us (6%)
    ppermute x3, waiting for transfers between devices, passed_along(): return lax.ppermute(value, axis, pairs)  855 us
    all_to_all x1, blocking collectives, on_device(): lax.all_to_all(spectra, 'freq', split_axis=0, concat_axis=1, tiled=True)  101 us
    broadcast_in_dim x1, local copies, waits for them, and re-layouts, on_device(): return jnp.stack(tile_list, axis=1)[:, None]  74.7 us
    dot_general x1, matrix products, on_device(): jnp.einsum('qpcr,qimp->cirm', fourier_table(points, CHAN), frames, precis...  69.3 us
    dot_general x5, matrix products, cross_tile(): jnp.einsum('...at,...nbt->...anb', left_rows, stacked, preferred_element_...  65.4 us
    another operation x5, other arithmetic, cross_tile(): jnp.stack([jnp.concatenate([real_part, imag_part], -1), jnp.concatenate([...  38 us
    convert_element_type x1, local copies, waits for them, and re-layouts, on_device(): voltages.reshape(2, in_dev, frames_total, points).astype(jnp.float32)  28.8 us
  transfers between devices with their start and end apart: 3, of which 2 were waited for; matrix products, arithmetic and copies ran while one was open for 6% of the time, Pallas kernels for 0%

commit v1 on v0

--- a/solution.py
+++ b/solution.py
@@ -1,14 +1,22 @@
+import functools
 import math
 
 import jax
 import jax.numpy as jnp
+import numpy as np
 from jax import lax
+from jax.experimental import pallas as pl
+from jax.experimental.pallas import tpu as pltpu
 from jax.sharding import PartitionSpec as P
 
 CHAN = 128
 
 
 spectrum_scale = 1.0 / 128.0
+
+LANES = 128
+CHUNKS = (8, 8, 8, 8)
+ROWS_EACH = ((((1,), (1,)), ((), ())))
 
 
 def passed_along(value, axis, steps):
@@ -48,7 +56,7 @@
     return (product * (1.0 / spectra_len)).astype(jnp.bfloat16)
 
 
-def on_device(voltages, window_taps):
+def on_device_any(voltages, window_taps):
     taps_count, points = window_taps.shape
     in_dev = voltages.shape[2]
     frames_total = voltages.shape[3] // points
@@ -58,11 +66,9 @@
     spectra = jnp.einsum(
         "qpcr,qimp->cirm", fourier_table(points, CHAN), frames, precision=lax.Precision.HIGHEST
     ).astype(jnp.bfloat16)
-    blocks = lax.axis_size("tri")
-    half_count = blocks // 2
+    half_count = lax.axis_size("tri") // 2
     own_block = lax.all_to_all(spectra, "freq", split_axis=0, concat_axis=1, tiled=True)
-    group_chans = own_block.shape[0]
-    block_len = own_block.shape[1]
+    group_chans, block_len = own_block.shape[:2]
     left_rows = own_block.reshape(group_chans, block_len, 2 * spectra_len)
     held = own_block[None]
     while held.shape[0] < half_count + 1:
@@ -70,23 +76,376 @@
         count = min(run_len, half_count + 1 - run_len)
         received = passed_along(held[:count], "tri", -run_len)
         held = jnp.concatenate([held, received], 0)
-
-    def fetch_block(offset):
-        return held[offset]
-
-    tile_list = [cross_tile(left_rows, own_block)]
-    for offset in range(1, half_count):
-        tile_list.append(cross_tile(left_rows, fetch_block(offset)))
-    far_block = fetch_block(half_count)
-    full_tile = cross_tile(left_rows, far_block)
-    tile_list.append(full_tile)
+    tile_list = [cross_tile(left_rows, held[offset]) for offset in range(half_count + 1)]
     return jnp.stack(tile_list, axis=1)[:, None]
+
+
+def table_rows(points, chans):
+    phase = (np.arange(points)[:, None] * np.arange(chans)[None, :] % points).astype(np.float64)
+    phase = phase * (2.0 * math.pi / points)
+    cosine, sine = np.cos(phase), np.sin(phase)
+    real_row = np.concatenate([cosine, sine], 0).T
+    imag_row = np.concatenate([-sine, cosine], 0).T
+    return (np.stack([real_row, imag_row], 0) * spectrum_scale).astype(np.float32)
+
+
+def channelize_kernel(chunks, spectra_len, volt_ref, taps_ref, table_ref, *refs):
+    n_out = 3 * len(chunks)
+    outs = refs[:n_out]
+    frames_ref, spec_ref = refs[n_out:]
+    points = taps_ref.shape[1]
+    taps_count = taps_ref.shape[0] // 8
+    lane_parts = points // LANES
+    group = volt_ref.shape[2]
+    total_chans = table_ref.shape[0] // 4
+    n_rows = 2 * total_chans
+
+    for sub in range(group // 8):
+        for q in range(2):
+            for part in range(lane_parts):
+                weight = [
+                    taps_ref[8 * k : 8 * k + 8, part * LANES : (part + 1) * LANES]
+                    for k in range(taps_count)
+                ]
+
+                def sample(m, q=q, part=part, sub=sub):
+                    start = pl.multiple_of(m * points + part * LANES, LANES)
+                    return volt_ref[q, 0, 8 * sub : 8 * sub + 8, pl.ds(start, LANES)].astype(jnp.float32)
+
+                step = 8
+
+                def body(i, carry, weight=weight, sample=sample, q=q, part=part):
+                    held = list(carry)
+                    for r in range(step):
+                        m = i * step + r
+                        held.append(sample(m + taps_count - 1))
+                        total = held[0] * weight[0]
+                        for k in range(1, taps_count):
+                            total = total + held[k] * weight[k]
+                        held = held[1:]
+                        row = pl.multiple_of(m * 8, 8)
+                        frames_ref[q * lane_parts + part, pl.ds(row, 8), :] = total
+                    return tuple(held)
+
+                lax.fori_loop(
+                    0, spectra_len // step, body, tuple(sample(k) for k in range(taps_count - 1))
+                )
+
+        def one_input(n, carry, sub=sub):
+            frame = jnp.concatenate(
+                [
+                    frames_ref[part, pl.ds(n, spectra_len, stride=8), :]
+                    for part in range(2 * lane_parts)
+                ],
+                axis=1,
+            )
+            high = frame.astype(jnp.bfloat16)
+            low = (frame - high.astype(jnp.float32)).astype(jnp.bfloat16)
+            first = lax.dot_general(
+                table_ref[0 : 2 * n_rows, :], high, ROWS_EACH, preferred_element_type=jnp.float32
+            )
+            second = lax.dot_general(
+                table_ref[0:n_rows, :], low, ROWS_EACH, preferred_element_type=jnp.float32
+            )
+            spec = first[:n_rows] + (first[n_rows:] + second)
+            for ri in range(2):
+                for part in range(spectra_len // LANES):
+                    spec_ref[
+                        ri * (spectra_len // LANES) + part,
+                        pl.ds(sub * 8 + n, total_chans, stride=group),
+                        :,
+                    ] = spec[
+                        ri * total_chans : (ri + 1) * total_chans, part * LANES : (part + 1) * LANES
+                    ]
+            return carry
+
+        lax.fori_loop(0, 8, one_input, 0)
+
+    group_chans = sum(chunks)
+    n_parts = 2 * spectra_len // LANES
+    start = 0
+    for k, count in enumerate(chunks):
+        near, across, paired = outs[3 * k : 3 * k + 3]
+        for j, target in ((0, near), (2, across), (1, paired.at[0]), (3, paired.at[1])):
+            base = (j * group_chans + start) * group
+            for part in range(n_parts):
+                piece = spec_ref[part, base : base + count * group, :].astype(jnp.bfloat16)
+                target[:, :, part * LANES : (part + 1) * LANES] = piece.reshape(count, group, LANES)
+        start += count
+
+
+def channelize(voltages, window_taps, table, chunks):
+    taps_count, points = window_taps.shape
+    in_dev, samples = voltages.shape[2:]
+    spectra_len = samples // points - taps_count + 1
+    group = 16
+    wide = 2 * spectra_len
+    chans = table.shape[0] // 4
+    taps = jnp.repeat(window_taps, 8, axis=0)
+    shapes, specs = [], []
+    for count in chunks:
+        for lead in ((), (), (2,)):
+            shapes.append(jax.ShapeDtypeStruct(lead + (count, in_dev, wide), jnp.bfloat16))
+            zero = (0,) * (len(lead) + 1)
+            specs.append(
+                pl.BlockSpec(lead + (count, group, wide), lambda i, zero=zero: zero + (i, 0))
+            )
+    return pl.pallas_call(
+        functools.partial(channelize_kernel, chunks, spectra_len),
+        grid=(in_dev // group,),
+        in_specs=[
+            pl.BlockSpec((2, 1, group, samples), lambda i: (0, 0, i, 0)),
+            pl.BlockSpec(taps.shape, lambda i: (0, 0)),
+            pl.BlockSpec(table.shape, lambda i: (0, 0)),
+        ],
+        out_specs=specs,
+        out_shape=shapes,
+        scratch_shapes=[
+            pltpu.VMEM((2 * points // LANES, 8 * spectra_len, LANES), jnp.float32),
+            pltpu.VMEM((wide // LANES, chans * group, LANES), jnp.float32),
+        ],
+        compiler_params=pltpu.CompilerParams(vmem_limit_bytes=56 << 20),
+        cost_estimate=pl.CostEstimate(
+            flops=6 * in_dev * spectra_len * 2 * chans * 2 * points,
+            bytes_accessed=voltages.size * 4 + in_dev * wide * chans * 2,
+            transcendentals=0,
+        ),
+    )(voltages, taps, table)
+
+
+ROLES = ("own", "d1", "ua3", "d2", "u2", "xa_own", "xa_n2", "xb12", "xb3")
+
+
+def role_used(role, z, x):
+    return {
+        "own": 1,
+        "d1": jnp.where(z < 3, 1, 0),
+        "ua3": jnp.where(z == 3, 1, 0),
+        "d2": jnp.where(z < 2, 1, 0),
+        "u2": jnp.where(z >= 2, 1, 0),
+        "xa_own": 1 - x,
+        "xa_n2": x,
+        "xb12": jnp.where(z < 3, 1, 0),
+        "xb3": jnp.where(z == 3, 1, 0),
+    }[role]
+
+
+def correlate_kernel(scale, aliased, info_ref, *refs):
+    n_in = 2 * len(ROLES)
+    halves = [dict(zip(ROLES, refs[h * len(ROLES) : (h + 1) * len(ROLES)])) for h in range(2)]
+    out_ref, block_ref, left_ref = refs[n_in + (1 if aliased else 0) :]
+    f, z, x = info_ref[0], info_ref[1], info_ref[2]
+    rows = halves[0]["own"].shape[1] // 2
+    wide = halves[0]["own"].shape[2]
+    half_wide = wide // 2
+
+    def place(slot, role):
+        for h in range(2):
+            for sub in range(2):
+                at = pl.multiple_of((f ^ (2 * h + sub)) * rows, rows)
+                block_ref[slot, pl.ds(at, rows), :] = halves[h][role][
+                    0, sub * rows : (sub + 1) * rows, :
+                ]
+
+    place(0, "own")
+
+    @pl.when(x == 0)
+    def _():
+        place(1, "xa_own")
+
+    @pl.when(x == 1)
+    def _():
+        place(3, "xa_n2")
+
+    @pl.when(z < 3)
+    def _():
+        place(2, "d1")
+        place(3 - 2 * x, "xb12")
+
+    @pl.when(z == 3)
+    def _():
+        place(2, "ua3")
+        place(3 - 2 * x, "xb3")
+
+    @pl.when(z < 2)
+    def _():
+        place(4, "d2")
+
+    @pl.when(z >= 2)
+    def _():
+        place(4, "u2")
+
+    own = block_ref[0].astype(jnp.float32)
+    size = own.shape[0]
+    turned = jnp.concatenate([own[:, half_wide:], -own[:, :half_wide]], axis=1)
+    for part in range(wide // LANES):
+        cut = slice(part * LANES, (part + 1) * LANES)
+        left_ref[part, pl.ds(0, size, stride=2), :] = own[:, cut]
+        left_ref[part, pl.ds(1, size, stride=2), :] = turned[:, cut]
+    left = jnp.concatenate(
+        [left_ref[part].astype(jnp.bfloat16) for part in range(wide // LANES)], axis=1
+    )
+    for slot in range(5):
+        product = lax.dot_general(
+            left, block_ref[slot], ROWS_EACH, preferred_element_type=jnp.float32
+        )
+        out_ref[0, 0, slot] = (product * scale).astype(jnp.bfloat16).reshape(size, 2, size)
+
+
+def correlate(info, first, second, out, start, out_shape):
+    count, double_rows, wide = first["own"].shape
+    size = 2 * double_rows
+
+    def spec(role):
+        return pl.BlockSpec(
+            (1, double_rows, wide),
+            lambda c, info_ref: (c * role_used(role, info_ref[1], info_ref[2]), 0, 0),
+        )
+
+    operands = [half[role] for half in (first, second) for role in ROLES]
+    in_specs = [spec(role) for _ in range(2) for role in ROLES]
+    aliased = out is not None
+    aliases = {}
+    if aliased:
+        aliases = {1 + len(operands): 0}
+        operands.append(out)
+        in_specs.append(pl.BlockSpec(memory_space=pl.ANY))
+    offsets = out_shape.shape[2]
+    return pl.pallas_call(
+        functools.partial(correlate_kernel, 2.0 / wide, aliased),
+        grid_spec=pltpu.PrefetchScalarGridSpec(
+            num_scalar_prefetch=1,
+            grid=(count,),
+            in_specs=in_specs,
+            out_specs=pl.BlockSpec(
+                (1, 1, offsets, size, 2, size),
+                lambda c, info_ref: (c + start, 0, 0, 0, 0, 0),
+            ),
+            scratch_shapes=[
+                pltpu.VMEM((offsets, size, wide), jnp.bfloat16),
+                pltpu.VMEM((wide // LANES, 2 * size, LANES), jnp.float32),
+            ],
+        ),
+        out_shape=out_shape,
+        input_output_aliases=aliases,
+        compiler_params=pltpu.CompilerParams(vmem_limit_bytes=40 << 20),
+        cost_estimate=pl.CostEstimate(
+            flops=2 * count * offsets * 2 * size * size * wide,
+            bytes_accessed=count * offsets * size * (2 * size + wide) * 2,
+            transcendentals=0,
+        ),
+    )(info, *operands)
+
+
+def at(z, x):
+    return 2 * z + x
+
+
+DOWN = [(at(z + 1, x), at(z, x)) for z in range(3) for x in range(2)]
+DOWN_AGAIN = [(at(z + 1, x), at(z, x)) for z in range(2) for x in range(2)]
+UP_OWN = [(at(z, x), at(z + 1, x)) for z in range(2) for x in range(2)]
+UP_AGAIN = [(at(z, x), at(z + 1, x)) for z in (1, 2) for x in range(2)]
+UP_LAST = [(at(2, x), at(3, x)) for x in range(2)]
+SIDE_OWN = [(at(z, 1), at(z, 0)) for z in range(4)]
+SIDE_FAR = [(at(z, 0), at(z, 1)) for z in range(4)]
+SIDE_NEXT = [(at(z, x), at(z, 1 - x)) for z in range(3) for x in range(2)]
+SIDE_LAST = [(at(3, 0), at(3, 1)), (at(3, 1), at(3, 0))]
+
+
+def sent(value, pairs):
+    return lax.ppermute(value, "tri", pairs)
+
+
+def behind(value, *others):
+    return lax.optimization_barrier((value,) + others)[0]
+
+
+def spread(units, z, x):
+    got = []
+    for index in range(len(units) + 1):
+        last = got[index - 1] if index else None
+        if index == len(units):
+            far = jnp.where(z < 2, last["d2"], last["u2"])
+            last["ua3"] = sent(last["u2"], UP_LAST)
+            last["xa_n2"] = sent(far, SIDE_FAR)
+            last["xb3"] = sent(last["ua3"], SIDE_LAST)
+            break
+        now = {"own": units[index]}
+        got.append(now)
+        own = units[index]
+        if last is None:
+            up = sent(own, UP_OWN)
+            now["xa_own"] = sent(own, SIDE_OWN)
+        else:
+            own = behind(own, last["d2"], last["u2"], last["xa_own"], last["xb12"])
+            far = jnp.where(z < 2, last["d2"], last["u2"])
+            if last["own"].shape == own.shape:
+                up = sent(jnp.where(z == 2, last["u2"], own), UP_OWN + UP_LAST)
+                last["ua3"] = up
+                now["xa_own"] = last["xa_n2"] = sent(jnp.where(x == 1, own, far), SIDE_OWN + SIDE_FAR)
+            else:
+                up = sent(own, UP_OWN)
+                last["ua3"] = sent(last["u2"], UP_LAST)
+                now["xa_own"] = sent(own, SIDE_OWN)
+                last["xa_n2"] = sent(far, SIDE_FAR)
+        now["d1"] = sent(own, DOWN)
+        now["d2"] = sent(now["d1"], DOWN_AGAIN)
+        now["u2"] = sent(up, UP_AGAIN)
+        if last is not None and last["own"].shape == own.shape:
+            now["xb12"] = last["xb3"] = sent(
+                jnp.where(z == 3, up, now["d1"]), SIDE_NEXT + SIDE_LAST
+            )
+        else:
+            now["xb12"] = sent(now["d1"], SIDE_NEXT)
+            if last is not None:
+                last["xb3"] = sent(last["ua3"], SIDE_LAST)
+    return got
+
+
+def on_device(voltages, window_taps):
+    taps_count, points = window_taps.shape
+    in_dev = voltages.shape[2]
+    groups = lax.axis_size("freq")
+    group_chans = CHAN // groups
+    f = lax.axis_index("freq")
+    t = lax.axis_index("tri")
+    z, x = t // 2, t % 2
+    info = jnp.stack([f, z, x]).astype(jnp.int32)
+
+    exact = table_rows(points, CHAN)
+    high = exact.astype(jnp.bfloat16)
+    low = (exact - high.astype(np.float32)).astype(jnp.bfloat16)
+    table = jnp.asarray(np.stack([high, low], 0)).reshape(2, 2, groups, group_chans, 2 * points)
+    table = jnp.take(table, f ^ jnp.arange(groups), axis=2).reshape(4 * CHAN, 2 * points)
+
+    pieces = channelize(voltages, window_taps, table, CHUNKS)
+    chunk_count = len(CHUNKS)
+    other_core = [(g, g ^ 1) for g in range(groups)]
+    other_chip = [(g, g ^ 2) for g in range(groups)]
+    near_units, far_units = [], []
+    for k in range(chunk_count):
+        near, across, paired = pieces[3 * k : 3 * k + 3]
+        received = lax.ppermute(paired, "freq", other_core)
+        near_units.append(jnp.concatenate([near, received[0]], axis=1))
+        joined = jnp.concatenate([across, received[1]], axis=1)
+        far_units.append(lax.ppermute(joined, "freq", other_chip))
+
+    got = spread(near_units + far_units, z, x)
+    block = in_dev * groups
+    offsets = lax.axis_size("tri") // 2 + 1
+    out_shape = jax.ShapeDtypeStruct((group_chans, 1, offsets, block, 2, block), jnp.bfloat16)
+    out, start = None, 0
+    for k in range(chunk_count):
+        out = correlate(info, got[k], got[chunk_count + k], out, start, out_shape)
+        start += CHUNKS[k]
+    return out
 
 
 def solution(mesh):
     placed = (P(None, "tri", "freq", None), P())
+    small = mesh.shape["freq"] == 4 and mesh.shape["tri"] == 8
     return jax.shard_map(
-        on_device,
+        on_device if small else on_device_any,
         mesh=mesh,
         in_specs=placed,
         out_specs=P("freq", "tri", None, None, None, None),

time: 1360 us -> 604 us (0.44)
  waiting for transfers between devices: 855 us -> 348 us
  local copies, waits for them, and re-layouts: 183 us -> 30 us
  matrix products: 135 us -> 0 us
  Pallas kernels: 0 us -> 112 us
  blocking collectives: 101 us -> 0 us
  starting transfers between devices: 0.61 us -> 100 us
  other arithmetic: 83.9 us -> 9.57 us
    ppermute x3 -> x59, waiting for transfers between devices: 855 us -> 348 us  [the longest x51 345 us: sent(): return lax.ppermute(value, 'tri', pairs)]
    dot_general x6 -> x0, matrix products: 135 us -> none  [the longest x1 69.3 us: on_device(): jnp.einsum('qpcr,qimp->cirm', fourier_table(points, CHAN), frames, precis...]
    pallas_call x0 -> x5, Pallas kernels: none -> 112 us  [the longest x1 58.9 us: channelize(): pl.pallas_call(functools.partial(channelize_kernel, chunks, spectra_len),...]
    all_to_all x1 -> x0, blocking collectives: 101 us -> none  [on_device(): lax.all_to_all(spectra, 'freq', split_axis=0, concat_axis=1, tiled=True)]
    ppermute x3 -> x59, starting transfers between devices: 0.61 us -> 100 us  [the longest x51 95.2 us: sent(): return lax.ppermute(value, 'tri', pairs)]
    broadcast_in_dim x1 -> x2, local copies, waits for them, and re-layouts: 74.7 us -> 0.16 us  [on_device(): jnp.take(table, f ^ jnp.arange(groups), axis=2)]
    convert_element_type x2 -> x0, local copies, waits for them, and re-layouts: 49.8 us -> none  [the longest x1 28.8 us: on_device(): voltages.reshape(2, in_dev, frames_total, points).astype(jnp.float32)]
    another operation x6 -> x1, other arithmetic: 38.1 us -> 0.08 us  [on_device(): info = jnp.stack([f, z, x]).astype(jnp.int32)]
  transfers between devices with their start and end apart: 3 -> 59, of which waited for: 2 -> 35; matrix products, arithmetic and copies ran while one was open for 6% -> 1% of each run, Pallas kernels for 0% -> 7%
where the time goes in v1:
time: 604 us; the launch traced here: 601 us
  waiting for transfers between devices  348 us (58%)
  Pallas kernels  112 us (19%)
  starting transfers between devices  100 us (17%)
  local copies, waits for them, and re-layouts  30 us (5%)
  other arithmetic  9.57 us (2%)
    ppermute x51, waiting for transfers between devices, sent(): return lax.ppermute(value, 'tri', pairs)  345 us
    ppermute x51, starting transfers between devices, sent(): return lax.ppermute(value, 'tri', pairs)  95.2 us
    pallas_call x1, Pallas kernels, channelize(): pl.pallas_call(functools.partial(channelize_kernel, chunks, spectra_len),...  58.9 us
    pallas_call x4, Pallas kernels, correlate(): pl.pallas_call(functools.partial(correlate_kernel, 2.0 / wide, aliased),...  53.1 us
    unnamed x166, local copies, waits for them, and re-layouts  24.4 us
  transfers between devices with their start and end apart: 59, of which 35 were waited for; matrix products, arithmetic and copies ran while one was open for 1% of the time, Pallas kernels for 7%

profile of v1, /device:TPU:26, one launch (start us, length us, event | category | flops | bytes accessed | tf_op | source)
XLA Modules:
  0.0 601.3 jit_solution(8381192242141498370)
XLA Ops:
  3.4 58.9 %shard_map.37 = (bf16[8,64,512]{2,1,0:T(8,128)(2,1)}, bf16[8,64,512]{2,1,0:T(8,128)(2,1)}, bf16[2,8,64,512]{3,2,1,0:T(8,128)(2,1)}, bf16[8,64,512]{2,1,0:T(8,128...) custom-call(s32[2,1,64,66304]{3,2,1,0:T(8,128)} %volt_ref.1, ...), custom_call_target="tpu_custom_call" | custom-call | flops 12884901888 | bytes 42336256 | tf_op jit(solution)/shard_map/pallas_call | solution.py:193
  74.7 16.6 %collective-permute-done.4.refs_1_ = bf16[8,128,512]{2,1,0:T(8,128)(2,1)} collective-permute-done((bf16[8,128,512]{2,1,0:T(8,128)(2,1)S(1)}, bf16[8,128,512]{2,1,0:T(8,128)(2,1)}, u32[]{:S(2)}, u32[]{:S(2)}) %collective-permute-start.4) | collective-permute-done | bytes 1048608 | tf_op jit(solution)/shard_map/ppermute | solution.py:356
  96.7 26.3 %collective-permute-done.7.refs_4_ = bf16[8,128,512]{2,1,0:T(8,128)(2,1)} collective-permute-done((bf16[8,128,512]{2,1,0:T(8,128)(2,1)}, bf16[8,128,512]{2,1,0:T(8,128)(2,1)}, u32[]{:S(2)}, u32[]{:S(2)}) %collective-permute-start.7) | collective-permute-done | bytes 1048608 | tf_op jit(solution)/shard_map/ppermute | solution.py:356
  133.3 17.7 %collective-permute-done.12.refs_2_ = bf16[8,128,512]{2,1,0:T(8,128)(2,1)S(1)} collective-permute-done((bf16[8,128,512]{2,1,0:T(8,128)(2,1)}, bf16[8,128,512]{2,1,0:T(8,128)(2,1)S(1)}, u32[]{:S(2)}, u32[]{:S(2)}) %collective-permute-start.12) | collective-permute-done | bytes 1048608 | tf_op jit(solution)/shard_map/ppermute | solution.py:356
  158.0 22.0 %collective-permute-done.15.refs_8_.refs_7_ = bf16[8,128,512]{2,1,0:T(8,128)(2,1)S(1)} collective-permute-done((bf16[8,128,512]{2,1,0:T(8,128)(2,1)S(1)}, bf16[8,128,512]{2,1,0:T(8,128)(2,1)S(1)}, u32[]{:S(2)}, u32[]{:S(2)}) %collective-permute-start.15) | collective-permute-done | bytes 1048608 | tf_op jit(solution)/shard_map/ppermute | solution.py:356
  188.9 19.0 %collective-permute-done.18.refs_2_ = bf16[8,128,512]{2,1,0:T(8,128)(2,1)S(1)} collective-permute-done((bf16[8,128,512]{2,1,0:T(8,128)(2,1)S(1)}, bf16[8,128,512]{2,1,0:T(8,128)(2,1)S(1)}, u32[]{:S(2)}, u32[]{:S(2)}) %collective-permute-start.18) | collective-permute-done | bytes 1048608 | tf_op jit(solution)/shard_map/ppermute | solution.py:356
  213.4 22.0 %collective-permute-done.21.refs_8_.refs_7_ = bf16[8,128,512]{2,1,0:T(8,128)(2,1)S(1)} collective-permute-done((bf16[8,128,512]{2,1,0:T(8,128)(2,1)S(1)}, bf16[8,128,512]{2,1,0:T(8,128)(2,1)S(1)}, u32[]{:S(2)}, u32[]{:S(2)}) %collective-permute-start.21) | collective-permute-done | bytes 1048608 | tf_op jit(solution)/shard_map/ppermute | solution.py:356
  246.8 16.6 %collective-permute-done.23.refs_2_ = bf16[8,128,512]{2,1,0:T(8,128)(2,1)S(1)} collective-permute-done((bf16[8,128,512]{2,1,0:T(8,128)(2,1)S(1)}, bf16[8,128,512]{2,1,0:T(8,128)(2,1)S(1)}, u32[]{:S(2)}, u32[]{:S(2)}) %collective-permute-start.23) | collective-permute-done | bytes 1048608 | tf_op jit(solution)/shard_map/ppermute | solution.py:356
  271.8 19.0 %collective-permute-done.28.refs_8_.refs_7_ = bf16[8,128,512]{2,1,0:T(8,128)(2,1)S(1)} collective-permute-done((bf16[8,128,512]{2,1,0:T(8,128)(2,1)S(1)}, bf16[8,128,512]{2,1,0:T(8,128)(2,1)S(1)}, u32[]{:S(2)}, u32[]{:S(2)}) %collective-permute-start.28) | collective-permute-done | bytes 1048608 | tf_op jit(solution)/shard_map/ppermute | solution.py:356
  293.9 5.3 collective-permute-start.31
  301.3 15.3 %collective-permute-done.29.refs_2_ = bf16[8,128,512]{2,1,0:T(8,128)(2,1)S(1)} collective-permute-done((bf16[8,128,512]{2,1,0:T(8,128)(2,1)S(1)}, bf16[8,128,512]{2,1,0:T(8,128)(2,1)S(1)}, u32[]{:S(2)}, u32[]{:S(2)}) %collective-permute-start.29) | collective-permute-done | bytes 1048608 | tf_op jit(solution)/shard_map/ppermute | solution.py:356
  326.3 17.7 %collective-permute-done.32.refs_16_.refs_8_ = bf16[8,128,512]{2,1,0:T(8,128)(2,1)S(1)} collective-permute-done((bf16[8,128,512]{2,1,0:T(8,128)(2,1)S(1)}, bf16[8,128,512]{2,1,0:T(8,128)(2,1)S(1)}, u32[]{:S(2)}, u32[]{:S(2)}) %collective-permute-start.32) | collective-permute-done | bytes 1048608 | tf_op jit(solution)/shard_map/ppermute | solution.py:356
  353.8 14.9 %collective-permute-done.40.refs_11_ = bf16[8,128,512]{2,1,0:T(8,128)(2,1)S(1)} collective-permute-done((bf16[8,128,512]{2,1,0:T(8,128)(2,1)S(1)}, bf16[8,128,512]{2,1,0:T(8,128)(2,1)S(1)}, u32[]{:S(2)}, u32[]{:S(2)}) %collective-permute-start.40) | collective-permute-done | bytes 1048608 | tf_op jit(solution)/shard_map/ppermute | solution.py:356
  376.7 18.4 %collective-permute-done.43.refs_17_.refs_16_ = bf16[8,128,512]{2,1,0:T(8,128)(2,1)S(1)} collective-permute-done((bf16[8,128,512]{2,1,0:T(8,128)(2,1)S(1)}, bf16[8,128,512]{2,1,0:T(8,128)(2,1)S(1)}, u32[]{:S(2)}, u32[]{:S(2)}) %collective-permute-start.43) | collective-permute-done | bytes 1048608 | tf_op jit(solution)/shard_map/ppermute | solution.py:356
  406.7 14.5 %collective-permute-done.46.refs_11_ = bf16[8,128,512]{2,1,0:T(8,128)(2,1)S(1)} collective-permute-done((bf16[8,128,512]{2,1,0:T(8,128)(2,1)S(1)}, bf16[8,128,512]{2,1,0:T(8,128)(2,1)S(1)}, u32[]{:S(2)}, u32[]{:S(2)}) %collective-permute-start.46) | collective-permute-done | bytes 1048608 | tf_op jit(solution)/shard_map/ppermute | solution.py:356
  428.8 18.6 %collective-permute-done.49.refs_17_.refs_16_ = bf16[8,128,512]{2,1,0:T(8,128)(2,1)S(1)} collective-permute-done((bf16[8,128,512]{2,1,0:T(8,128)(2,1)S(1)}, bf16[8,128,512]{2,1,0:T(8,128)(2,1)S(1)}, u32[]{:S(2)}, u32[]{:S(2)}) %collective-permute-start.49) | collective-permute-done | bytes 1048608 | tf_op jit(solution)/shard_map/ppermute | solution.py:356
  456.0 18.1 %collective-permute-done.51.refs_11_ = bf16[8,128,512]{2,1,0:T(8,128)(2,1)S(1)} collective-permute-done((bf16[8,128,512]{2,1,0:T(8,128)(2,1)S(1)}, bf16[8,128,512]{2,1,0:T(8,128)(2,1)S(1)}, u32[]{:S(2)}, u32[]{:S(2)}) %collective-permute-start.51) | collective-permute-done | bytes 1048608 | tf_op jit(solution)/shard_map/ppermute | solution.py:356
  476.1 21.3 %collective-permute-done.52.refs_13_ = bf16[8,128,512]{2,1,0:T(8,128)(2,1)S(1)} collective-permute-done((bf16[8,128,512]{2,1,0:T(8,128)(2,1)S(1)}, bf16[8,128,512]{2,1,0:T(8,128)(2,1)S(1)}, u32[]{:S(2)}, u32[]{:S(2)}) %collective-permute-start.52) | collective-permute-done | bytes 1048608 | tf_op jit(solution)/shard_map/ppermute | solution.py:356
  505.6 14.1 %collective-permute-done.53.refs_11_ = bf16[8,128,512]{2,1,0:T(8,128)(2,1)} collective-permute-done((bf16[8,128,512]{2,1,0:T(8,128)(2,1)S(1)}, bf16[8,128,512]{2,1,0:T(8,128)(2,1)}, u32[]{:S(2)}, u32[]{:S(2)}) %collective-permute-start.53) | collective-permute-done | bytes 1048608 | tf_op jit(solution)/shard_map/ppermute | solution.py:356
  524.8 13.4 %shard_map.38.refs_18_ = bf16[32,1,5,256,2,256]{5,4,3,2,1,0:T(2,128)(2,1)} custom-call(s32[3]{0:T(128)S(1)} %pad_add_fusion.info_ref, bf16[8,128,512]{2,1,0:T(8,128)(2,1)S(1)} %copy-done.7, bf16[8,128,512]{2,1,0:T(8,128)(2,1)} %collective-permute-done.4.refs_1_, bf16[8,128,512]{2,1,0:T(8,128)(2,1)S(1)} %copy-done.11, bf16[8,128,512]{2,1,0:T(8,128)(2,1)S(1)} %copy-done.39, ...), custom_call_target="tpu_custom_call" | custom-call | flops 5368709120 | bytes 20971520 | tf_op jit(solution)/shard_map/pallas_call | solution.py:314
  544.3 13.3 %shard_map.39.refs_18_ = bf16[32,1,5,256,2,256]{5,4,3,2,1,0:T(2,128)(2,1)} custom-call(s32[3]{0:T(128)S(1)} %pad_add_fusion.info_ref, bf16[8,128,512]{2,1,0:T(8,128)(2,1)S(1)} %pad_maximum_fusion.2.refs_0_, bf16[8,128,512]{2,1,0:T(8,128)(2,1)S(1)} %copy-done.9, bf16[8,128,512]{2,1,0:T(8,128)(2,1)S(1)} %copy-done.15, ...), custom_call_target="tpu_custom_call", output_to_operand_aliasing={{}: (19, {})} | custom-call | flops 5368709120 | bytes 20971520 | tf_op jit(solution)/shard_map/pallas_call | solution.py:314
  564.1 13.2 %shard_map.40.refs_18_ = bf16[32,1,5,256,2,256]{5,4,3,2,1,0:T(2,128)(2,1)} custom-call(s32[3]{0:T(128)S(1)} %pad_add_fusion.info_ref, bf16[8,128,512]{2,1,0:T(8,128)(2,1)S(1)} %pad_maximum_fusion.1.refs_0_, bf16[8,128,512]{2,1,0:T(8,128)(2,1)S(1)} %copy-done.13, bf16[8,128,512]{2,1,0:T(8,128)(2,1)S(1)} %copy-done.19, ...), custom_call_target="tpu_custom_call", output_to_operand_aliasing={{}: (19, {})} | custom-call | flops 5368709120 | bytes 20971520 | tf_op jit(solution)/shard_map/pallas_call | solution.py:314
  577.3 9.5 %collective-permute-done.58.refs_17_ = bf16[8,128,512]{2,1,0:T(8,128)(2,1)} collective-permute-done((bf16[8,128,512]{2,1,0:T(8,128)(2,1)}, bf16[8,128,512]{2,1,0:T(8,128)(2,1)}, u32[]{:S(2)}, u32[]{:S(2)}) %collective-permute-start.58) | collective-permute-done | bytes 1048608 | tf_op jit(solution)/shard_map/ppermute | solution.py:356
  588.1 13.2 %shard_map.41 = bf16[32,1,5,256,2,256]{5,4,3,2,1,0:T(2,128)(2,1)} custom-call(s32[3]{0:T(128)S(1)} %pad_add_fusion.info_ref, bf16[8,128,512]{2,1,0:T(8,128)(2,1)S(1)} %pad_maximum_fusion.refs_0_, bf16[8,128,512]{2,1,0:T(8,128)(2,1)S(1)} %copy-done.17, bf16[8,128,512]{2,1,0:T(8,128)(2,1)S(1)} %copy-done.21, ...), custom_call_target="tpu_custom_call", output_to_operand_aliasing={{}: (19, {})} | custom-call | flops 5368709120 | bytes 20971520 | tf_op jit(solution)/shard_map/pallas_call | solution.py:314
  (302 shorter events, 161.2 us)
Async XLA Ops:
  71.2 25.5 %collective-permute-start.8 = (bf16[8,128,512]{2,1,0:T(8,128)(2,1)S(1)}, bf16[8,128,512]{2,1,0:T(8,128)(2,1)}, u32[]{:S(2)}, u32[]{:S(2)}) collective-permute-start(bf16[8,128,512]{2,1,0:T(8,128)(2,1)S(1)} %pad_maximum_fusion.3.refs_0_), channel_id=1, source_target_pairs={{1,0},{3,2},{5,4},{7,6},{9,8},{11,10},{13,12},{15,14},{17,16},{19,... | collective-permute-start | bytes 3145736 | tf_op jit(solution)/shard_map/ppermute | solution.py:356
  93.8 29.3 %collective-permute-start.7 = (bf16[8,128,512]{2,1,0:T(8,128)(2,1)}, bf16[8,128,512]{2,1,0:T(8,128)(2,1)}, u32[]{:S(2)}, u32[]{:S(2)}) collective-permute-start(bf16[8,128,512]{2,1,0:T(8,128)(2,1)} %collective-permute-done.6), channel_id=1, source_target_pairs={{2,4},{3,5},{4,6},{5,7},{10,12},{11,13},{12,14},{13,15},{18,20},{1... | collective-permute-start | bytes 3145736 | tf_op jit(solution)/shard_map/ppermute | solution.py:356
  125.8 25.3 %collective-permute-start.12 = (bf16[8,128,512]{2,1,0:T(8,128)(2,1)}, bf16[8,128,512]{2,1,0:T(8,128)(2,1)S(1)}, u32[]{:S(2)}, u32[]{:S(2)}) collective-permute-start(bf16[8,128,512]{2,1,0:T(8,128)(2,1)} %get-tuple-element.56), channel_id=1, source_target_pairs={{0,2},{1,3},{2,4},{3,5},{4,6},{5,7},{8,10},{9,11},{10,12},{11,13},... | collective-permute-start | bytes 3145736 | tf_op jit(solution)/shard_map/ppermute | solution.py:356
  131.8 26.2 %collective-permute-start.14 = (bf16[8,128,512]{2,1,0:T(8,128)(2,1)}, bf16[8,128,512]{2,1,0:T(8,128)(2,1)S(1)}, u32[]{:S(2)}, u32[]{:S(2)}) collective-permute-start(bf16[8,128,512]{2,1,0:T(8,128)(2,1)} %get-tuple-element.55), channel_id=1, source_target_pairs={{1,0},{3,2},{5,4},{7,6},{0,1},{2,3},{4,5},{6,7},{9,8},{11,10},{13,... | collective-permute-start | bytes 3145736 | tf_op jit(solution)/shard_map/ppermute | solution.py:356
  152.1 27.9 %collective-permute-start.15 = (bf16[8,128,512]{2,1,0:T(8,128)(2,1)S(1)}, bf16[8,128,512]{2,1,0:T(8,128)(2,1)S(1)}, u32[]{:S(2)}, u32[]{:S(2)}) collective-permute-start(bf16[8,128,512]{2,1,0:T(8,128)(2,1)S(1)} %broadcast_select_fusion.6), channel_id=1, source_target_pairs={{0,1},{1,0},{2,3},{3,2},{4,5},{5,4},{6,7},{7,6},{8,9},{9,8},{10,11... | collective-permute-start | bytes 3145736 | tf_op jit(solution)/shard_map/ppermute | solution.py:356
  153.7 26.3 %collective-permute-start.13 = (bf16[8,128,512]{2,1,0:T(8,128)(2,1)S(1)}, bf16[8,128,512]{2,1,0:T(8,128)(2,1)S(1)}, u32[]{:S(2)}, u32[]{:S(2)}) collective-permute-start(bf16[8,128,512]{2,1,0:T(8,128)(2,1)S(1)} %collective-permute-done.12.refs_2_), channel_id=1, source_target_pairs={{2,4},{3,5},{4,6},{5,7},{10,12},{11,13},{12,14},{13,15},{18,20},{1... | collective-permute-start | bytes 3145736 | tf_op jit(solution)/shard_map/ppermute | solution.py:356
  181.3 26.6 %collective-permute-start.18 = (bf16[8,128,512]{2,1,0:T(8,128)(2,1)S(1)}, bf16[8,128,512]{2,1,0:T(8,128)(2,1)S(1)}, u32[]{:S(2)}, u32[]{:S(2)}) collective-permute-start(bf16[8,128,512]{2,1,0:T(8,128)(2,1)S(1)} %get-tuple-element.54), channel_id=1, source_target_pairs={{0,2},{1,3},{2,4},{3,5},{4,6},{5,7},{8,10},{9,11},{10,12},{11,13},... | collective-permute-start | bytes 3145736 | tf_op jit(solution)/shard_map/ppermute | solution.py:356
  182.6 26.5 %collective-permute-start.16 = (bf16[8,128,512]{2,1,0:T(8,128)(2,1)S(1)}, bf16[8,128,512]{2,1,0:T(8,128)(2,1)S(1)}, u32[]{:S(2)}, u32[]{:S(2)}) collective-permute-start(bf16[8,128,512]{2,1,0:T(8,128)(2,1)S(1)} %pad_maximum_fusion.1.refs_0_), channel_id=1, source_target_pairs={{2,0},{3,1},{4,2},{5,3},{6,4},{7,5},{10,8},{11,9},{12,10},{13,11},... | collective-permute-start | bytes 3145736 | tf_op jit(solution)/shard_map/ppermute | solution.py:356
  187.3 25.6 %collective-permute-start = (bf16[2,8,64,512]{3,2,1,0:T(8,128)(2,1)S(1)}, bf16[2,8,64,512]{3,2,1,0:T(8,128)(2,1)S(1)}, u32[]{:S(2)}, u32[]{:S(2)}) collective-permute-start(bf16[2,8,64,512]{3,2,1,0:T(8,128)(2,1)S(1)} %copy-done.82), channel_id=1, source_target_pairs={{0,8},{8,0},{16,24},{24,16},{1,9},{9,1},{17,25},{25,17},{2,10},{10... | collective-permute-start | bytes 3145736 | tf_op jit(solution)/shard_map/ppermute | solution.py:428
  187.3 26.0 %collective-permute-start.20 = (bf16[8,128,512]{2,1,0:T(8,128)(2,1)S(1)}, bf16[8,128,512]{2,1,0:T(8,128)(2,1)S(1)}, u32[]{:S(2)}, u32[]{:S(2)}) collective-permute-start(bf16[8,128,512]{2,1,0:T(8,128)(2,1)S(1)} %get-tuple-element.53), channel_id=1, source_target_pairs={{1,0},{3,2},{5,4},{7,6},{0,1},{2,3},{4,5},{6,7},{9,8},{11,10},{13,... | collective-permute-start | bytes 3145736 | tf_op jit(solution)/shard_map/ppermute | solution.py:356
  209.2 26.1 %collective-permute-start.21 = (bf16[8,128,512]{2,1,0:T(8,128)(2,1)S(1)}, bf16[8,128,512]{2,1,0:T(8,128)(2,1)S(1)}, u32[]{:S(2)}, u32[]{:S(2)}) collective-permute-start(bf16[8,128,512]{2,1,0:T(8,128)(2,1)S(1)} %broadcast_select_fusion.5), channel_id=1, source_target_pairs={{0,1},{1,0},{2,3},{3,2},{4,5},{5,4},{6,7},{7,6},{8,9},{9,8},{10,11... | collective-permute-start | bytes 3145736 | tf_op jit(solution)/shard_map/ppermute | solution.py:356
  210.8 25.9 %collective-permute-start.19 = (bf16[8,128,512]{2,1,0:T(8,128)(2,1)S(1)}, bf16[8,128,512]{2,1,0:T(8,128)(2,1)S(1)}, u32[]{:S(2)}, u32[]{:S(2)}) collective-permute-start(bf16[8,128,512]{2,1,0:T(8,128)(2,1)S(1)} %collective-permute-done.18.refs_2_), channel_id=1, source_target_pairs={{2,4},{3,5},{4,6},{5,7},{10,12},{11,13},{12,14},{13,15},{18,20},{1... | collective-permute-start | bytes 3145736 | tf_op jit(solution)/shard_map/ppermute | solution.py:356
  238.1 25.3 %collective-permute-start.23 = (bf16[8,128,512]{2,1,0:T(8,128)(2,1)S(1)}, bf16[8,128,512]{2,1,0:T(8,128)(2,1)S(1)}, u32[]{:S(2)}, u32[]{:S(2)}) collective-permute-start(bf16[8,128,512]{2,1,0:T(8,128)(2,1)S(1)} %get-tuple-element.52), channel_id=1, source_target_pairs={{0,2},{1,3},{2,4},{3,5},{4,6},{5,7},{8,10},{9,11},{10,12},{11,13},... | collective-permute-start | bytes 3145736 | tf_op jit(solution)/shard_map/ppermute | solution.py:356
  239.4 25.2 %collective-permute-start.22 = (bf16[8,128,512]{2,1,0:T(8,128)(2,1)S(1)}, bf16[8,128,512]{2,1,0:T(8,128)(2,1)S(1)}, u32[]{:S(2)}, u32[]{:S(2)}) collective-permute-start(bf16[8,128,512]{2,1,0:T(8,128)(2,1)S(1)} %pad_maximum_fusion.refs_0_), channel_id=1, source_target_pairs={{2,0},{3,1},{4,2},{5,3},{6,4},{7,5},{10,8},{11,9},{12,10},{13,11},... | collective-permute-start | bytes 3145736 | tf_op jit(solution)/shard_map/ppermute | solution.py:356
  246.2 25.6 %collective-permute-start.27 = (bf16[8,128,512]{2,1,0:T(8,128)(2,1)S(1)}, bf16[8,128,512]{2,1,0:T(8,128)(2,1)S(1)}, u32[]{:S(2)}, u32[]{:S(2)}) collective-permute-start(bf16[8,128,512]{2,1,0:T(8,128)(2,1)S(1)} %get-tuple-element.51), channel_id=1, source_target_pairs={{1,0},{3,2},{5,4},{7,6},{0,1},{2,3},{4,5},{6,7},{9,8},{11,10},{13,... | collective-permute-start | bytes 3145736 | tf_op jit(solution)/shard_map/ppermute | solution.py:356
  264.7 26.1 %collective-permute-start.28 = (bf16[8,128,512]{2,1,0:T(8,128)(2,1)S(1)}, bf16[8,128,512]{2,1,0:T(8,128)(2,1)S(1)}, u32[]{:S(2)}, u32[]{:S(2)}) collective-permute-start(bf16[8,128,512]{2,1,0:T(8,128)(2,1)S(1)} %broadcast_select_fusion.4), channel_id=1, source_target_pairs={{0,1},{1,0},{2,3},{3,2},{4,5},{5,4},{6,7},{7,6},{8,9},{9,8},{10,11... | collective-permute-start | bytes 3145736 | tf_op jit(solution)/shard_map/ppermute | solution.py:356
  300.9 25.4 %collective-permute-start.30 = (bf16[8,128,512]{2,1,0:T(8,128)(2,1)S(1)}, bf16[8,128,512]{2,1,0:T(8,128)(2,1)S(1)}, u32[]{:S(2)}, u32[]{:S(2)}) collective-permute-start(bf16[8,128,512]{2,1,0:T(8,128)(2,1)S(1)} %get-tuple-element.49), channel_id=1, source_target_pairs={{1,0},{3,2},{5,4},{7,6},{0,1},{2,3},{4,5},{6,7},{9,8},{11,10},{13,... | collective-permute-start | bytes 3145736 | tf_op jit(solution)/shard_map/ppermute | solution.py:356
  318.0 26.0 %collective-permute-start.32 = (bf16[8,128,512]{2,1,0:T(8,128)(2,1)S(1)}, bf16[8,128,512]{2,1,0:T(8,128)(2,1)S(1)}, u32[]{:S(2)}, u32[]{:S(2)}) collective-permute-start(bf16[8,128,512]{2,1,0:T(8,128)(2,1)S(1)} %broadcast_select_fusion.3), channel_id=1, source_target_pairs={{0,1},{1,0},{2,3},{3,2},{4,5},{5,4},{6,7},{7,6},{8,9},{9,8},{10,11... | collective-permute-start | bytes 3145736 | tf_op jit(solution)/shard_map/ppermute | solution.py:356
  370.0 25.1 %collective-permute-start.43 = (bf16[8,128,512]{2,1,0:T(8,128)(2,1)S(1)}, bf16[8,128,512]{2,1,0:T(8,128)(2,1)S(1)}, u32[]{:S(2)}, u32[]{:S(2)}) collective-permute-start(bf16[8,128,512]{2,1,0:T(8,128)(2,1)S(1)} %broadcast_select_fusion.2), channel_id=1, source_target_pairs={{0,1},{1,0},{2,3},{3,2},{4,5},{5,4},{6,7},{7,6},{8,9},{9,8},{10,11... | collective-permute-start | bytes 3145736 | tf_op jit(solution)/shard_map/ppermute | solution.py:356
  475.3 27.5 %collective-permute-start.54 = (bf16[8,128,512]{2,1,0:T(8,128)(2,1)S(1)}, bf16[8,128,512]{2,1,0:T(8,128)(2,1)S(1)}, u32[]{:S(2)}, u32[]{:S(2)}) collective-permute-start(bf16[8,128,512]{2,1,0:T(8,128)(2,1)S(1)} %collective-permute-done.50.refs_10_), channel_id=1, source_target_pairs={{2,0},{3,1},{4,2},{5,3},{10,8},{11,9},{12,10},{13,11},{18,16},{19,... | collective-permute-start | bytes 3145736 | tf_op jit(solution)/shard_map/ppermute | solution.py:356
  498.7 58.9 %collective-permute-start.55 = (bf16[8,128,512]{2,1,0:T(8,128)(2,1)}, bf16[8,128,512]{2,1,0:T(8,128)(2,1)}, u32[]{:S(2)}, u32[]{:S(2)}) collective-permute-start(bf16[8,128,512]{2,1,0:T(8,128)(2,1)} %get-tuple-element.43), channel_id=1, source_target_pairs={{1,0},{3,2},{5,4},{7,6},{0,1},{2,3},{4,5},{6,7},{9,8},{11,10},{13,... | collective-permute-start | bytes 3145736 | tf_op jit(solution)/shard_map/ppermute | solution.py:356
  502.6 55.1 %collective-permute-start.57 = (bf16[8,128,512]{2,1,0:T(8,128)(2,1)}, bf16[8,128,512]{2,1,0:T(8,128)(2,1)}, u32[]{:S(2)}, u32[]{:S(2)}) collective-permute-start(bf16[8,128,512]{2,1,0:T(8,128)(2,1)} %broadcast_select_fusion), channel_id=1, source_target_pairs={{0,1},{1,0},{2,3},{3,2},{4,5},{5,4},{6,7},{7,6},{8,9},{9,8},{10,11... | collective-permute-start | bytes 3145736 | tf_op jit(solution)/shard_map/ppermute | solution.py:356
  504.0 73.3 %collective-permute-start.56 = (bf16[8,128,512]{2,1,0:T(8,128)(2,1)}, bf16[8,128,512]{2,1,0:T(8,128)(2,1)}, u32[]{:S(2)}, u32[]{:S(2)}) collective-permute-start(bf16[8,128,512]{2,1,0:T(8,128)(2,1)} %broadcast_select_fusion.7), channel_id=1, source_target_pairs={{0,1},{2,3},{4,5},{6,7},{8,9},{10,11},{12,13},{14,15},{16,17},{18,... | collective-permute-start | bytes 3145736 | tf_op jit(solution)/shard_map/ppermute | solution.py:356
  519.6 67.1 %collective-permute-start.58 = (bf16[8,128,512]{2,1,0:T(8,128)(2,1)}, bf16[8,128,512]{2,1,0:T(8,128)(2,1)}, u32[]{:S(2)}, u32[]{:S(2)}) collective-permute-start(bf16[8,128,512]{2,1,0:T(8,128)(2,1)} %collective-permute-done.53.refs_11_), channel_id=1, source_target_pairs={{6,7},{7,6},{14,15},{15,14},{22,23},{23,22},{30,31},{31,30}} | collective-permute-start | bytes 3145736 | tf_op jit(solution)/shard_map/ppermute | solution.py:356
  (118 other events, 1941.2 us)

commit v2 on v1

--- a/solution.py
+++ b/solution.py
@@ -15,7 +15,10 @@
 spectrum_scale = 1.0 / 128.0
 
 LANES = 128
-CHUNKS = (8, 8, 8, 8)
+CHUNKS = (4,) * 8
+STREAMS = 2
+LEAD = 2
+DELAY = 100
 ROWS_EACH = ((((1,), (1,)), ((), ())))
 
 
@@ -101,35 +104,42 @@
     n_rows = 2 * total_chans
 
     for sub in range(group // 8):
-        for q in range(2):
-            for part in range(lane_parts):
-                weight = [
-                    taps_ref[8 * k : 8 * k + 8, part * LANES : (part + 1) * LANES]
-                    for k in range(taps_count)
-                ]
-
-                def sample(m, q=q, part=part, sub=sub):
-                    start = pl.multiple_of(m * points + part * LANES, LANES)
-                    return volt_ref[q, 0, 8 * sub : 8 * sub + 8, pl.ds(start, LANES)].astype(jnp.float32)
-
-                step = 8
-
-                def body(i, carry, weight=weight, sample=sample, q=q, part=part):
-                    held = list(carry)
-                    for r in range(step):
-                        m = i * step + r
-                        held.append(sample(m + taps_count - 1))
-                        total = held[0] * weight[0]
+        weight = [
+            [
+                taps_ref[8 * k : 8 * k + 8, part * LANES : (part + 1) * LANES]
+                for k in range(taps_count)
+            ]
+            for part in range(lane_parts)
+        ]
+
+        def sample(m, q, part, sub=sub):
+            start = pl.multiple_of(m * points + part * LANES, LANES)
+            return volt_ref[q, 0, 8 * sub : 8 * sub + 8, pl.ds(start, LANES)].astype(jnp.float32)
+
+        step = 8
+
+        def body(i, carry, weight=weight, sample=sample):
+            held = [list(c) for c in carry]
+            for r in range(step):
+                m = i * step + r
+                row = pl.multiple_of(m * 8, 8)
+                for q in range(2):
+                    for part in range(lane_parts):
+                        which = q * lane_parts + part
+                        now = held[which] + [sample(m + taps_count - 1, q, part)]
+                        total = now[0] * weight[part][0]
                         for k in range(1, taps_count):
-                            total = total + held[k] * weight[k]
-                        held = held[1:]
-                        row = pl.multiple_of(m * 8, 8)
-                        frames_ref[q * lane_parts + part, pl.ds(row, 8), :] = total
-                    return tuple(held)
-
-                lax.fori_loop(
-                    0, spectra_len // step, body, tuple(sample(k) for k in range(taps_count - 1))
-                )
+                            total = total + now[k] * weight[part][k]
+                        held[which] = now[1:]
+                        frames_ref[which, pl.ds(row, 8), :] = total
+            return tuple(tuple(h) for h in held)
+
+        first_samples = tuple(
+            tuple(sample(k, q, part) for k in range(taps_count - 1))
+            for q in range(2)
+            for part in range(lane_parts)
+        )
+        lax.fori_loop(0, spectra_len // step, body, first_samples)
 
         def one_input(n, carry, sub=sub):
             frame = jnp.concatenate(
@@ -159,7 +169,7 @@
                     ]
             return carry
 
-        lax.fori_loop(0, 8, one_input, 0)
+        lax.fori_loop(0, 8, one_input, 0, unroll=True)
 
     group_chans = sum(chunks)
     n_parts = 2 * spectra_len // LANES
@@ -233,7 +243,8 @@
 def correlate_kernel(scale, aliased, info_ref, *refs):
     n_in = 2 * len(ROLES)
     halves = [dict(zip(ROLES, refs[h * len(ROLES) : (h + 1) * len(ROLES)])) for h in range(2)]
-    out_ref, block_ref, left_ref = refs[n_in + (1 if aliased else 0) :]
+    out_ref, token_ref, block_ref, left_ref = refs[n_in + (1 if aliased else 0) :]
+    token_ref[...] = jnp.zeros_like(token_ref)
     f, z, x = info_ref[0], info_ref[1], info_ref[2]
     rows = halves[0]["own"].shape[1] // 2
     wide = halves[0]["own"].shape[2]
@@ -317,18 +328,21 @@
             num_scalar_prefetch=1,
             grid=(count,),
             in_specs=in_specs,
-            out_specs=pl.BlockSpec(
-                (1, 1, offsets, size, 2, size),
-                lambda c, info_ref: (c + start, 0, 0, 0, 0, 0),
-            ),
+            out_specs=[
+                pl.BlockSpec(
+                    (1, 1, offsets, size, 2, size),
+                    lambda c, info_ref: (c + start, 0, 0, 0, 0, 0),
+                ),
+                pl.BlockSpec((8, LANES), lambda c, info_ref: (0, 0)),
+            ],
             scratch_shapes=[
                 pltpu.VMEM((offsets, size, wide), jnp.bfloat16),
                 pltpu.VMEM((wide // LANES, 2 * size, LANES), jnp.float32),
             ],
         ),
-        out_shape=out_shape,
+        out_shape=[out_shape, jax.ShapeDtypeStruct((8, LANES), jnp.int32)],
         input_output_aliases=aliases,
-        compiler_params=pltpu.CompilerParams(vmem_limit_bytes=40 << 20),
+        compiler_params=pltpu.CompilerParams(vmem_limit_bytes=60 << 20),
         cost_estimate=pl.CostEstimate(
             flops=2 * count * offsets * 2 * size * size * wide,
             bytes_accessed=count * offsets * size * (2 * size + wide) * 2,
@@ -360,45 +374,43 @@
     return lax.optimization_barrier((value,) + others)[0]
 
 
-def spread(units, z, x):
+def spread(units, z, x, gate_on):
     got = []
-    for index in range(len(units) + 1):
-        last = got[index - 1] if index else None
-        if index == len(units):
+    for index in range(len(units) + STREAMS):
+        past = index - STREAMS
+        last = got[past] if past >= 0 else None
+        if last is not None:
             far = jnp.where(z < 2, last["d2"], last["u2"])
+        if index >= len(units):
             last["ua3"] = sent(last["u2"], UP_LAST)
             last["xa_n2"] = sent(far, SIDE_FAR)
-            last["xb3"] = sent(last["ua3"], SIDE_LAST)
-            break
-        now = {"own": units[index]}
+            last["xb3"] = sent(behind(last["ua3"], last["xa_n2"]), SIDE_LAST)
+            continue
+        own = units[index]
+        now = {"own": own}
         got.append(now)
-        own = units[index]
         if last is None:
             up = sent(own, UP_OWN)
             now["xa_own"] = sent(own, SIDE_OWN)
         else:
             own = behind(own, last["d2"], last["u2"], last["xa_own"], last["xb12"])
-            far = jnp.where(z < 2, last["d2"], last["u2"])
-            if last["own"].shape == own.shape:
-                up = sent(jnp.where(z == 2, last["u2"], own), UP_OWN + UP_LAST)
-                last["ua3"] = up
-                now["xa_own"] = last["xa_n2"] = sent(jnp.where(x == 1, own, far), SIDE_OWN + SIDE_FAR)
-            else:
-                up = sent(own, UP_OWN)
-                last["ua3"] = sent(last["u2"], UP_LAST)
-                now["xa_own"] = sent(own, SIDE_OWN)
-                last["xa_n2"] = sent(far, SIDE_FAR)
+            late = gate_on(index, got)
+            up = last["ua3"] = sent(jnp.where(z + late == 2, last["u2"], own), UP_OWN + UP_LAST)
+            now["xa_own"] = last["xa_n2"] = sent(
+                jnp.where(x + late == 1, own, far), SIDE_OWN + SIDE_FAR
+            )
         now["d1"] = sent(own, DOWN)
-        now["d2"] = sent(now["d1"], DOWN_AGAIN)
+        down = now["d1"]
+        if index >= len(units) - STREAMS:
+            down = behind(down, up, now["xa_own"])
+        now["d2"] = sent(down, DOWN_AGAIN)
         now["u2"] = sent(up, UP_AGAIN)
-        if last is not None and last["own"].shape == own.shape:
+        if last is None:
+            now["xb12"] = sent(now["d1"], SIDE_NEXT)
+        else:
             now["xb12"] = last["xb3"] = sent(
                 jnp.where(z == 3, up, now["d1"]), SIDE_NEXT + SIDE_LAST
             )
-        else:
-            now["xb12"] = sent(now["d1"], SIDE_NEXT)
-            if last is not None:
-                last["xb3"] = sent(last["ua3"], SIDE_LAST)
     return got
 
 
@@ -430,15 +442,33 @@
         joined = jnp.concatenate([across, received[1]], axis=1)
         far_units.append(lax.ppermute(joined, "freq", other_chip))
 
-    got = spread(near_units + far_units, z, x)
+    order = [(0, k) for k in range(LEAD)]
+    for k in range(chunk_count):
+        order += [(1, k)] + ([(0, k + LEAD)] if k + LEAD < chunk_count else [])
+    place = {unit: index for index, unit in enumerate(order)}
     block = in_dev * groups
     offsets = lax.axis_size("tri") // 2 + 1
     out_shape = jax.ShapeDtypeStruct((group_chans, 1, offsets, block, 2, block), jnp.bfloat16)
-    out, start = None, 0
-    for k in range(chunk_count):
-        out = correlate(info, got[k], got[chunk_count + k], out, start, out_shape)
-        start += CHUNKS[k]
-    return out
+    state = {"out": None, "next": 0}
+
+    def correlate_next(got):
+        k = state["next"]
+        state["out"], token = correlate(
+            info, got[place[0, k]], got[place[1, k]], state["out"], sum(CHUNKS[:k]), out_shape
+        )
+        state["next"] = k + 1
+        return token
+
+    def gate_on(index, got):
+        token = jnp.int32(0)
+        while state["next"] < chunk_count and place[1, state["next"]] + DELAY <= index:
+            token = correlate_next(got)[0, 0]
+        return token
+
+    got = spread([(near_units, far_units)[h][k] for h, k in order], z, x, gate_on)
+    while state["next"] < chunk_count:
+        correlate_next(got)
+    return state["out"]
 
 
 def solution(mesh):

time: 604 us -> 561 us (0.929)
  waiting for transfers between devices: 348 us -> 213 us
  starting transfers between devices: 100 us -> 193 us
  local copies, waits for them, and re-layouts: 30 us -> 8.23 us
  other arithmetic: 9.57 us -> 27.1 us
    ppermute x51 -> x102, waiting for transfers between devices: 345 us -> 209 us  [sent(): return lax.ppermute(value, 'tri', pairs)]
    ppermute x51 -> x102, starting transfers between devices: 95.2 us -> 182 us  [sent(): return lax.ppermute(value, 'tri', pairs)]
    pallas_call x1, Pallas kernels: 58.9 us -> 36.7 us  [channelize(): pl.pallas_call(functools.partial(channelize_kernel, chunks, spectra_len),...]
    unnamed x166 -> x204, local copies, waits for them, and re-layouts: 24.4 us -> 4.46 us
    pallas_call x4 -> x8, Pallas kernels: 53.1 us -> 72.1 us  [correlate(): pl.pallas_call(functools.partial(correlate_kernel, 2.0 / wide, aliased),...]
    concatenate x4 -> x8, other arithmetic: 0.3 us -> 6.96 us  [on_device(): near_units.append(jnp.concatenate([near, received[0]], axis=1))]
  transfers between devices with their start and end apart: 59 -> 118, of which waited for: 35 -> 47; matrix products, arithmetic and copies ran while one was open for 1% -> 5% of each run, Pallas kernels for 7% -> 11%
where the time goes in v2:
time: 561 us; the launch traced here: 552 us
  waiting for transfers between devices  213 us (38%)
  starting transfers between devices  193 us (34%)
  Pallas kernels  109 us (19%)
  other arithmetic  27.1 us (5%)
  local copies, waits for them, and re-layouts  8.23 us (1%)
    ppermute x102, waiting for transfers between devices, sent(): return lax.ppermute(value, 'tri', pairs)  209 us
    ppermute x102, starting transfers between devices, sent(): return lax.ppermute(value, 'tri', pairs)  182 us
    pallas_call x8, Pallas kernels, correlate(): pl.pallas_call(functools.partial(correlate_kernel, 2.0 / wide, aliased),...  72.1 us
    pallas_call x1, Pallas kernels, channelize(): pl.pallas_call(functools.partial(channelize_kernel, chunks, spectra_len),...  36.7 us
  transfers between devices with their start and end apart: 118, of which 47 were waited for; matrix products, arithmetic and copies ran while one was open for 5% of the time, Pallas kernels for 11%

profile of v2, /device:TPU:26, one launch (start us, length us, event | category | flops | bytes accessed | tf_op | source)
XLA Modules:
  0.0 552.4 jit_solution(2317149623597070514)
XLA Ops:
  3.4 36.7 %shard_map.37 = (bf16[4,64,512]{2,1,0:T(8,128)(2,1)}, bf16[4,64,512]{2,1,0:T(8,128)(2,1)}, bf16[2,4,64,512]{3,2,1,0:T(8,128)(2,1)}, bf16[4,64,512]{2,1,0:T(8,128...) custom-call(s32[2,1,64,66304]{3,2,1,0:T(8,128)} %volt_ref.1, ...), custom_call_target="tpu_custom_call" | custom-call | flops 12884901888 | bytes 42336256 | tf_op jit(solution)/shard_map/pallas_call | solution.py:203
  83.3 12.2 %collective-permute-start.73 = (bf16[4,128,512]{2,1,0:T(8,128)(2,1)}, bf16[4,128,512]{2,1,0:T(8,128)(2,1)}, u32[]{:S(2)}, u32[]{:S(2)}) collective-permute-start(bf16[4,128,512]{2,1,0:T(8,128)(2,1)} %collective-permute-done.66.refs_9_), channel_id=1, source_target_pairs={{2,0},{3,1},{4,2},{5,3},{6,4},{7,5},{10,8},{11,9},{12,10},{13,11},... | collective-permute-start | bytes 1572872 | tf_op jit(solution)/shard_map/ppermute | solution.py:370
  100.5 6.8 %collective-permute-start.13 = (bf16[4,128,512]{2,1,0:T(8,128)(2,1)S(1)}, bf16[4,128,512]{2,1,0:T(8,128)(2,1)S(1)}, u32[]{:S(2)}, u32[]{:S(2)}) collective-permute-start(bf16[4,128,512]{2,1,0:T(8,128)(2,1)S(1)} %pad_maximum_fusion.5.refs_0_), channel_id=1, source_target_pairs={{2,0},{3,1},{4,2},{5,3},{6,4},{7,5},{10,8},{11,9},{12,10},{13,11},... | collective-permute-start | bytes 1572872 | tf_op jit(solution)/shard_map/ppermute | solution.py:370
  130.4 10.0 %collective-permute-done.78.refs_8_.refs_16_ = bf16[4,128,512]{2,1,0:T(8,128)(2,1)} collective-permute-done((bf16[4,128,512]{2,1,0:T(8,128)(2,1)S(1)}, bf16[4,128,512]{2,1,0:T(8,128)(2,1)}, u32[]{:S(2)}, u32[]{:S(2)}) %collective-permute-start.78) | collective-permute-done | bytes 524320 | tf_op jit(solution)/shard_map/ppermute | solution.py:370
  163.4 7.1 %collective-permute-done.81.refs_11_ = bf16[4,128,512]{2,1,0:T(8,128)(2,1)S(1)} collective-permute-done((bf16[4,128,512]{2,1,0:T(8,128)(2,1)S(1)}, bf16[4,128,512]{2,1,0:T(8,128)(2,1)S(1)}, u32[]{:S(2)}, u32[]{:S(2)}) %collective-permute-start.81) | collective-permute-done | bytes 524320 | tf_op jit(solution)/shard_map/ppermute | solution.py:370
  187.6 9.5 %collective-permute-done.84.refs_17_.refs_16_ = bf16[4,128,512]{2,1,0:T(8,128)(2,1)S(1)} collective-permute-done((bf16[4,128,512]{2,1,0:T(8,128)(2,1)S(1)}, bf16[4,128,512]{2,1,0:T(8,128)(2,1)S(1)}, u32[]{:S(2)}, u32[]{:S(2)}) %collective-permute-start.84) | collective-permute-done | bytes 524320 | tf_op jit(solution)/shard_map/ppermute | solution.py:370
  220.9 6.3 %collective-permute-done.87.refs_11_ = bf16[4,128,512]{2,1,0:T(8,128)(2,1)S(1)} collective-permute-done((bf16[4,128,512]{2,1,0:T(8,128)(2,1)S(1)}, bf16[4,128,512]{2,1,0:T(8,128)(2,1)S(1)}, u32[]{:S(2)}, u32[]{:S(2)}) %collective-permute-start.87) | collective-permute-done | bytes 524320 | tf_op jit(solution)/shard_map/ppermute | solution.py:370
  245.3 8.7 %collective-permute-done.90.refs_17_.refs_16_ = bf16[4,128,512]{2,1,0:T(8,128)(2,1)S(1)} collective-permute-done((bf16[4,128,512]{2,1,0:T(8,128)(2,1)S(1)}, bf16[4,128,512]{2,1,0:T(8,128)(2,1)S(1)}, u32[]{:S(2)}, u32[]{:S(2)}) %collective-permute-start.90) | collective-permute-done | bytes 524320 | tf_op jit(solution)/shard_map/ppermute | solution.py:370
  274.2 7.8 %collective-permute-done.93.refs_11_ = bf16[4,128,512]{2,1,0:T(8,128)(2,1)S(1)} collective-permute-done((bf16[4,128,512]{2,1,0:T(8,128)(2,1)S(1)}, bf16[4,128,512]{2,1,0:T(8,128)(2,1)S(1)}, u32[]{:S(2)}, u32[]{:S(2)}) %collective-permute-start.93) | collective-permute-done | bytes 524320 | tf_op jit(solution)/shard_map/ppermute | solution.py:370
  299.9 9.5 %collective-permute-done.96.refs_17_.refs_16_ = bf16[4,128,512]{2,1,0:T(8,128)(2,1)S(1)} collective-permute-done((bf16[4,128,512]{2,1,0:T(8,128)(2,1)S(1)}, bf16[4,128,512]{2,1,0:T(8,128)(2,1)S(1)}, u32[]{:S(2)}, u32[]{:S(2)}) %collective-permute-start.96) | collective-permute-done | bytes 524320 | tf_op jit(solution)/shard_map/ppermute | solution.py:370
  331.7 8.0 %collective-permute-done.99.refs_11_ = bf16[4,128,512]{2,1,0:T(8,128)(2,1)S(1)} collective-permute-done((bf16[4,128,512]{2,1,0:T(8,128)(2,1)S(1)}, bf16[4,128,512]{2,1,0:T(8,128)(2,1)S(1)}, u32[]{:S(2)}, u32[]{:S(2)}) %collective-permute-start.99) | collective-permute-done | bytes 524320 | tf_op jit(solution)/shard_map/ppermute | solution.py:370
  357.6 8.6 %collective-permute-done.102.refs_17_.refs_16_ = bf16[4,128,512]{2,1,0:T(8,128)(2,1)S(1)} collective-permute-done((bf16[4,128,512]{2,1,0:T(8,128)(2,1)S(1)}, bf16[4,128,512]{2,1,0:T(8,128)(2,1)S(1)}, u32[]{:S(2)}, u32[]{:S(2)}) %collective-permute-start.102) | collective-permute-done | bytes 524320 | tf_op jit(solution)/shard_map/ppermute | solution.py:370
  386.7 7.5 %collective-permute-done.105.refs_11_ = bf16[4,128,512]{2,1,0:T(8,128)(2,1)S(1)} collective-permute-done((bf16[4,128,512]{2,1,0:T(8,128)(2,1)S(1)}, bf16[4,128,512]{2,1,0:T(8,128)(2,1)S(1)}, u32[]{:S(2)}, u32[]{:S(2)}) %collective-permute-start.105) | collective-permute-done | bytes 524320 | tf_op jit(solution)/shard_map/ppermute | solution.py:370
  397.7 7.7 %collective-permute-done.44.refs_2_ = bf16[4,128,512]{2,1,0:T(8,128)(2,1)S(1)} collective-permute-done((bf16[4,128,512]{2,1,0:T(8,128)(2,1)S(1)}, bf16[4,128,512]{2,1,0:T(8,128)(2,1)S(1)}, u32[]{:S(2)}, u32[]{:S(2)}) %collective-permute-start.44) | collective-permute-done | bytes 524320 | tf_op jit(solution)/shard_map/ppermute | solution.py:370
  410.8 9.4 %collective-permute-done.108.refs_17_.refs_16_ = bf16[4,128,512]{2,1,0:T(8,128)(2,1)S(1)} collective-permute-done((bf16[4,128,512]{2,1,0:T(8,128)(2,1)S(1)}, bf16[4,128,512]{2,1,0:T(8,128)(2,1)S(1)}, u32[]{:S(2)}, u32[]{:S(2)}) %collective-permute-start.108) | collective-permute-done | bytes 524320 | tf_op jit(solution)/shard_map/ppermute | solution.py:370
  433.0 6.9 %collective-permute-done.49.refs_8_.refs_7_ = bf16[4,128,512]{2,1,0:T(8,128)(2,1)S(1)} collective-permute-done((bf16[4,128,512]{2,1,0:T(8,128)(2,1)S(1)}, bf16[4,128,512]{2,1,0:T(8,128)(2,1)S(1)}, u32[]{:S(2)}, u32[]{:S(2)}) %collective-permute-start.49) | collective-permute-done | bytes 524320 | tf_op jit(solution)/shard_map/ppermute | solution.py:370
  454.8 9.3 %shard_map.38 = (bf16[32,1,5,256,2,256]{5,4,3,2,1,0:T(2,128)(2,1)}, s32[8,128]{1,0:T(8,128)}) custom-call(s32[3]{0:T(128)} %pad_add_fusion.info_ref, bf16[4,128,512]{2,1,0:T(8,128)(2,1)} %copy-done.83, bf16[4,128,512]{2,1,0:T(8,128)(2,1)} %collective-permute-done.67.refs_1_, bf16[4,128,512]{2,1,0:T(8,128)(2,1)} %collective-permute-done.75.refs_2_, ...), custom_call_target="tpu_custom_call" | custom-call | flops 2684354560 | bytes 10485760 | tf_op jit(solution)/shard_map/pallas_call | solution.py:325
  466.3 9.0 %shard_map.39 = (bf16[32,1,5,256,2,256]{5,4,3,2,1,0:T(2,128)(2,1)}, s32[8,128]{1,0:T(8,128)}) custom-call(s32[3]{0:T(128)} %pad_add_fusion.info_ref, bf16[4,128,512]{2,1,0:T(8,128)(2,1)} %copy-done.8, bf16[4,128,512]{2,1,0:T(8,128)(2,1)} %copy-done.88, bf16[4,128,512]{2,1,0:T(8,128)(2,1)} %copy-done.10, ...), custom_call_target="tpu_custom_call", output_to_operand_aliasing={{0}: (19, {})} | custom-call | flops 2684354560 | bytes 10485760 | tf_op jit(solution)/shard_map/pallas_call | solution.py:325
  475.4 9.0 %shard_map.40 = (bf16[32,1,5,256,2,256]{5,4,3,2,1,0:T(2,128)(2,1)}, s32[8,128]{1,0:T(8,128)}) custom-call(s32[3]{0:T(128)} %pad_add_fusion.info_ref, bf16[4,128,512]{2,1,0:T(8,128)(2,1)} %copy-done.2, bf16[4,128,512]{2,1,0:T(8,128)(2,1)} %copy-done.9, bf16[4,128,512]{2,1,0:T(8,128)(2,1)} %copy-done.13, ...), custom_call_target="tpu_custom_call", output_to_operand_aliasing={{0}: (19, {})} | custom-call | flops 2684354560 | bytes 10485760 | tf_op jit(solution)/shard_map/pallas_call | solution.py:325
  495.9 8.9 %shard_map.41 = (bf16[32,1,5,256,2,256]{5,4,3,2,1,0:T(2,128)(2,1)}, s32[8,128]{1,0:T(8,128)}) custom-call(s32[3]{0:T(128)} %pad_add_fusion.info_ref, bf16[4,128,512]{2,1,0:T(8,128)(2,1)} %copy-done.3, bf16[4,128,512]{2,1,0:T(8,128)(2,1)} %copy-done.11, bf16[4,128,512]{2,1,0:T(8,128)(2,1)} %copy-done.15, ...), custom_call_target="tpu_custom_call", output_to_operand_aliasing={{0}: (19, {})} | custom-call | flops 2684354560 | bytes 10485760 | tf_op jit(solution)/shard_map/pallas_call | solution.py:325
  514.1 9.0 %shard_map.42 = (bf16[32,1,5,256,2,256]{5,4,3,2,1,0:T(2,128)(2,1)}, s32[8,128]{1,0:T(8,128)}) custom-call(s32[3]{0:T(128)} %pad_add_fusion.info_ref, bf16[4,128,512]{2,1,0:T(8,128)(2,1)} %copy-done.4, bf16[4,128,512]{2,1,0:T(8,128)(2,1)} %copy-done.14, bf16[4,128,512]{2,1,0:T(8,128)(2,1)} %copy-done.19, ...), custom_call_target="tpu_custom_call", output_to_operand_aliasing={{0}: (19, {})} | custom-call | flops 2684354560 | bytes 10485760 | tf_op jit(solution)/shard_map/pallas_call | solution.py:325
  524.2 8.9 %shard_map.43 = (bf16[32,1,5,256,2,256]{5,4,3,2,1,0:T(2,128)(2,1)}, s32[8,128]{1,0:T(8,128)}) custom-call(s32[3]{0:T(128)} %pad_add_fusion.info_ref, bf16[4,128,512]{2,1,0:T(8,128)(2,1)} %copy-done.5, bf16[4,128,512]{2,1,0:T(8,128)(2,1)} %copy-done.18, bf16[4,128,512]{2,1,0:T(8,128)(2,1)} %copy-done.23, ...), custom_call_target="tpu_custom_call", output_to_operand_aliasing={{0}: (19, {})} | custom-call | flops 2684354560 | bytes 10485760 | tf_op jit(solution)/shard_map/pallas_call | solution.py:325
  533.2 9.0 %shard_map.44 = (bf16[32,1,5,256,2,256]{5,4,3,2,1,0:T(2,128)(2,1)}, s32[8,128]{1,0:T(8,128)}) custom-call(s32[3]{0:T(128)} %pad_add_fusion.info_ref, bf16[4,128,512]{2,1,0:T(8,128)(2,1)} %copy-done.6, bf16[4,128,512]{2,1,0:T(8,128)(2,1)} %copy-done.22, bf16[4,128,512]{2,1,0:T(8,128)(2,1)} %copy-done.27, ...), custom_call_target="tpu_custom_call", output_to_operand_aliasing={{0}: (19, {})} | custom-call | flops 2684354560 | bytes 10485760 | tf_op jit(solution)/shard_map/pallas_call | solution.py:325
  543.1 9.1 %shard_map.45 = (bf16[32,1,5,256,2,256]{5,4,3,2,1,0:T(2,128)(2,1)}, s32[8,128]{1,0:T(8,128)}) custom-call(s32[3]{0:T(128)} %pad_add_fusion.info_ref, bf16[4,128,512]{2,1,0:T(8,128)(2,1)} %copy-done.7, bf16[4,128,512]{2,1,0:T(8,128)(2,1)} %copy-done.26, bf16[4,128,512]{2,1,0:T(8,128)(2,1)} %collective-permute-done.50.refs_2_, ...), custom_call_target="tpu_custom_call", output_to_operand_aliasing={{0}: (19, {})} | custom-call | flops 2684354560 | bytes 10485760 | tf_op jit(solution)/shard_map/pallas_call | solution.py:325
  (489 shorter events, 315.1 us)
Async XLA Ops:
  70.9 24.5 %collective-permute-start.8 = (bf16[4,128,512]{2,1,0:T(8,128)(2,1)}, bf16[4,128,512]{2,1,0:T(8,128)(2,1)S(1)}, u32[]{:S(2)}, u32[]{:S(2)}) collective-permute-start(bf16[4,128,512]{2,1,0:T(8,128)(2,1)} %copy-done.88), channel_id=1, source_target_pairs={{2,0},{3,1},{4,2},{5,3},{10,8},{11,9},{12,10},{13,11},{18,16},{19,... | collective-permute-start | bytes 1572872 | tf_op jit(solution)/shard_map/ppermute | solution.py:370
  71.6 25.1 %collective-permute-start.12 = (bf16[4,128,512]{2,1,0:T(8,128)(2,1)}, bf16[4,128,512]{2,1,0:T(8,128)(2,1)S(1)}, u32[]{:S(2)}, u32[]{:S(2)}) collective-permute-start(bf16[4,128,512]{2,1,0:T(8,128)(2,1)} %copy-done.88), channel_id=1, source_target_pairs={{0,1},{1,0},{2,3},{3,2},{4,5},{5,4},{8,9},{9,8},{10,11},{11,10},{1... | collective-permute-start | bytes 1572872 | tf_op jit(solution)/shard_map/ppermute | solution.py:370
  72.4 24.4 %collective-permute-start.10 = (bf16[4,128,512]{2,1,0:T(8,128)(2,1)}, bf16[4,128,512]{2,1,0:T(8,128)(2,1)S(1)}, u32[]{:S(2)}, u32[]{:S(2)}) collective-permute-start(bf16[4,128,512]{2,1,0:T(8,128)(2,1)} %collective-permute-done.9), channel_id=1, source_target_pairs={{2,4},{3,5},{4,6},{5,7},{10,12},{11,13},{12,14},{13,15},{18,20},{1... | collective-permute-start | bytes 1572872 | tf_op jit(solution)/shard_map/ppermute | solution.py:370
  80.9 35.5 %collective-permute-start.4 = (bf16[2,4,64,512]{3,2,1,0:T(8,128)(2,1)}, bf16[2,4,64,512]{3,2,1,0:T(8,128)(2,1)}, u32[]{:S(2)}, u32[]{:S(2)}) collective-permute-start(bf16[2,4,64,512]{3,2,1,0:T(8,128)(2,1)} %get-tuple-element.64), channel_id=1, source_target_pairs={{0,8},{8,0},{16,24},{24,16},{1,9},{9,1},{17,25},{25,17},{2,10},{10... | collective-permute-start | bytes 1572872 | tf_op jit(solution)/shard_map/ppermute | solution.py:440
  83.3 30.8 %collective-permute-start.73 = (bf16[4,128,512]{2,1,0:T(8,128)(2,1)}, bf16[4,128,512]{2,1,0:T(8,128)(2,1)}, u32[]{:S(2)}, u32[]{:S(2)}) collective-permute-start(bf16[4,128,512]{2,1,0:T(8,128)(2,1)} %collective-permute-done.66.refs_9_), channel_id=1, source_target_pairs={{2,0},{3,1},{4,2},{5,3},{6,4},{7,5},{10,8},{11,9},{12,10},{13,11},... | collective-permute-start | bytes 1572872 | tf_op jit(solution)/shard_map/ppermute | solution.py:370
  121.7 26.6 %collective-permute-start.17 = (bf16[4,128,512]{2,1,0:T(8,128)(2,1)}, bf16[4,128,512]{2,1,0:T(8,128)(2,1)}, u32[]{:S(2)}, u32[]{:S(2)}) collective-permute-start(bf16[4,128,512]{2,1,0:T(8,128)(2,1)} %get-tuple-element.131), channel_id=1, source_target_pairs={{1,0},{3,2},{5,4},{7,6},{0,1},{2,3},{4,5},{6,7},{9,8},{11,10},{13,... | collective-permute-start | bytes 1572872 | tf_op jit(solution)/shard_map/ppermute | solution.py:370
  129.1 24.6 %collective-permute-start.18 = (bf16[4,128,512]{2,1,0:T(8,128)(2,1)S(1)}, bf16[4,128,512]{2,1,0:T(8,128)(2,1)S(1)}, u32[]{:S(2)}, u32[]{:S(2)}) collective-permute-start(bf16[4,128,512]{2,1,0:T(8,128)(2,1)S(1)} %broadcast_select_fusion.13), channel_id=1, source_target_pairs={{0,1},{1,0},{2,3},{3,2},{4,5},{5,4},{6,7},{7,6},{8,9},{9,8},{10,11... | collective-permute-start | bytes 1572872 | tf_op jit(solution)/shard_map/ppermute | solution.py:370
  144.6 28.2 %collective-permute-start.3 = (bf16[2,4,64,512]{3,2,1,0:T(8,128)(2,1)}, bf16[2,4,64,512]{3,2,1,0:T(8,128)(2,1)S(1)}, u32[]{:S(2)}, u32[]{:S(2)}) collective-permute-start(bf16[2,4,64,512]{3,2,1,0:T(8,128)(2,1)} %get-tuple-element.62), channel_id=1, source_target_pairs={{0,8},{8,0},{16,24},{24,16},{1,9},{9,1},{17,25},{25,17},{2,10},{10... | collective-permute-start | bytes 1572872 | tf_op jit(solution)/shard_map/ppermute | solution.py:440
  180.0 25.5 %collective-permute-start.23 = (bf16[4,128,512]{2,1,0:T(8,128)(2,1)S(1)}, bf16[4,128,512]{2,1,0:T(8,128)(2,1)S(1)}, u32[]{:S(2)}, u32[]{:S(2)}) collective-permute-start(bf16[4,128,512]{2,1,0:T(8,128)(2,1)S(1)} %get-tuple-element.129), channel_id=1, source_target_pairs={{1,0},{3,2},{5,4},{7,6},{0,1},{2,3},{4,5},{6,7},{9,8},{11,10},{13,... | collective-permute-start | bytes 1572872 | tf_op jit(solution)/shard_map/ppermute | solution.py:370
  185.9 25.2 %collective-permute-start.24 = (bf16[4,128,512]{2,1,0:T(8,128)(2,1)S(1)}, bf16[4,128,512]{2,1,0:T(8,128)(2,1)S(1)}, u32[]{:S(2)}, u32[]{:S(2)}) collective-permute-start(bf16[4,128,512]{2,1,0:T(8,128)(2,1)S(1)} %broadcast_select_fusion.12), channel_id=1, source_target_pairs={{0,1},{1,0},{2,3},{3,2},{4,5},{5,4},{6,7},{7,6},{8,9},{9,8},{10,11... | collective-permute-start | bytes 1572872 | tf_op jit(solution)/shard_map/ppermute | solution.py:370
  200.2 30.3 %collective-permute-start.2 = (bf16[2,4,64,512]{3,2,1,0:T(8,128)(2,1)}, bf16[2,4,64,512]{3,2,1,0:T(8,128)(2,1)S(1)}, u32[]{:S(2)}, u32[]{:S(2)}) collective-permute-start(bf16[2,4,64,512]{3,2,1,0:T(8,128)(2,1)} %get-tuple-element.60), channel_id=1, source_target_pairs={{0,8},{8,0},{16,24},{24,16},{1,9},{9,1},{17,25},{25,17},{2,10},{10... | collective-permute-start | bytes 1572872 | tf_op jit(solution)/shard_map/ppermute | solution.py:440
  257.1 28.0 %collective-permute-start.1 = (bf16[2,4,64,512]{3,2,1,0:T(8,128)(2,1)}, bf16[2,4,64,512]{3,2,1,0:T(8,128)(2,1)S(1)}, u32[]{:S(2)}, u32[]{:S(2)}) collective-permute-start(bf16[2,4,64,512]{3,2,1,0:T(8,128)(2,1)} %get-tuple-element.58), channel_id=1, source_target_pairs={{0,8},{8,0},{16,24},{24,16},{1,9},{9,1},{17,25},{25,17},{2,10},{10... | collective-permute-start | bytes 1572872 | tf_op jit(solution)/shard_map/ppermute | solution.py:440
  291.9 26.1 %collective-permute-start.35 = (bf16[4,128,512]{2,1,0:T(8,128)(2,1)S(1)}, bf16[4,128,512]{2,1,0:T(8,128)(2,1)S(1)}, u32[]{:S(2)}, u32[]{:S(2)}) collective-permute-start(bf16[4,128,512]{2,1,0:T(8,128)(2,1)S(1)} %get-tuple-element.125), channel_id=1, source_target_pairs={{1,0},{3,2},{5,4},{7,6},{0,1},{2,3},{4,5},{6,7},{9,8},{11,10},{13,... | collective-permute-start | bytes 1572872 | tf_op jit(solution)/shard_map/ppermute | solution.py:370
  298.2 25.4 %collective-permute-start.36 = (bf16[4,128,512]{2,1,0:T(8,128)(2,1)S(1)}, bf16[4,128,512]{2,1,0:T(8,128)(2,1)S(1)}, u32[]{:S(2)}, u32[]{:S(2)}) collective-permute-start(bf16[4,128,512]{2,1,0:T(8,128)(2,1)S(1)} %broadcast_select_fusion.10), channel_id=1, source_target_pairs={{0,1},{1,0},{2,3},{3,2},{4,5},{5,4},{6,7},{7,6},{8,9},{9,8},{10,11... | collective-permute-start | bytes 1572872 | tf_op jit(solution)/shard_map/ppermute | solution.py:370
  312.5 30.4 %collective-permute-start = (bf16[2,4,64,512]{3,2,1,0:T(8,128)(2,1)}, bf16[2,4,64,512]{3,2,1,0:T(8,128)(2,1)S(1)}, u32[]{:S(2)}, u32[]{:S(2)}) collective-permute-start(bf16[2,4,64,512]{3,2,1,0:T(8,128)(2,1)} %get-tuple-element.56), channel_id=1, source_target_pairs={{0,8},{8,0},{16,24},{24,16},{1,9},{9,1},{17,25},{25,17},{2,10},{10... | collective-permute-start | bytes 1572872 | tf_op jit(solution)/shard_map/ppermute | solution.py:440
  368.4 28.0 %collective-permute-start.59 = (bf16[4,128,512]{2,1,0:T(8,128)(2,1)S(1)}, bf16[4,128,512]{2,1,0:T(8,128)(2,1)S(1)}, u32[]{:S(2)}, u32[]{:S(2)}) collective-permute-start(bf16[4,128,512]{2,1,0:T(8,128)(2,1)S(1)} %pad_maximum_fusion.8), channel_id=1, source_target_pairs={{0,16},{8,24},{16,0},{24,8},{1,17},{9,25},{17,1},{25,9},{2,18},{10... | collective-permute-start | bytes 1572872 | tf_op jit(solution)/shard_map/ppermute | solution.py:443
  380.8 24.6 %collective-permute-start.44 = (bf16[4,128,512]{2,1,0:T(8,128)(2,1)S(1)}, bf16[4,128,512]{2,1,0:T(8,128)(2,1)S(1)}, u32[]{:S(2)}, u32[]{:S(2)}) collective-permute-start(bf16[4,128,512]{2,1,0:T(8,128)(2,1)S(1)} %get-tuple-element.122), channel_id=1, source_target_pairs={{0,2},{1,3},{2,4},{3,5},{4,6},{5,7},{8,10},{9,11},{10,12},{11,13},... | collective-permute-start | bytes 1572872 | tf_op jit(solution)/shard_map/ppermute | solution.py:370
  396.4 25.6 %collective-permute-start.106 = (bf16[4,128,512]{2,1,0:T(8,128)(2,1)S(1)}, bf16[4,128,512]{2,1,0:T(8,128)(2,1)S(1)}, u32[]{:S(2)}, u32[]{:S(2)}) collective-permute-start(bf16[4,128,512]{2,1,0:T(8,128)(2,1)S(1)} %collective-permute-done.105.refs_11_), channel_id=1, source_target_pairs={{2,4},{3,5},{4,6},{5,7},{10,12},{11,13},{12,14},{13,15},{18,20},{1... | collective-permute-start | bytes 1572872 | tf_op jit(solution)/shard_map/ppermute | solution.py:370
  452.0 32.3 %collective-permute-start.114 = (bf16[4,128,512]{2,1,0:T(8,128)(2,1)}, bf16[4,128,512]{2,1,0:T(8,128)(2,1)}, u32[]{:S(2)}, u32[]{:S(2)}) collective-permute-start(bf16[4,128,512]{2,1,0:T(8,128)(2,1)} %collective-permute-done.109.refs_10_), channel_id=1, source_target_pairs={{2,0},{3,1},{4,2},{5,3},{10,8},{11,9},{12,10},{13,11},{18,16},{19,... | collective-permute-start | bytes 1572872 | tf_op jit(solution)/shard_map/ppermute | solution.py:370
  453.5 30.8 %collective-permute-start.111 = (bf16[4,128,512]{2,1,0:T(8,128)(2,1)}, bf16[4,128,512]{2,1,0:T(8,128)(2,1)}, u32[]{:S(2)}, u32[]{:S(2)}) collective-permute-start(bf16[4,128,512]{2,1,0:T(8,128)(2,1)} %collective-permute-done.110.refs_11_), channel_id=1, source_target_pairs={{2,4},{3,5},{4,6},{5,7},{10,12},{11,13},{12,14},{13,15},{18,20},{1... | collective-permute-start | bytes 1572872 | tf_op jit(solution)/shard_map/ppermute | solution.py:370
  493.1 30.3 %collective-permute-start.116 = (bf16[4,128,512]{2,1,0:T(8,128)(2,1)S(1)}, bf16[4,128,512]{2,1,0:T(8,128)(2,1)S(1)}, u32[]{:S(2)}, u32[]{:S(2)}) collective-permute-start(bf16[4,128,512]{2,1,0:T(8,128)(2,1)S(1)} %broadcast_select_fusion), channel_id=1, source_target_pairs={{0,1},{1,0},{2,3},{3,2},{4,5},{5,4},{6,7},{7,6},{8,9},{9,8},{10,11... | collective-permute-start | bytes 1572872 | tf_op jit(solution)/shard_map/ppermute | solution.py:370
  505.6 27.5 %collective-permute-start.117 = (bf16[4,128,512]{2,1,0:T(8,128)(2,1)}, bf16[4,128,512]{2,1,0:T(8,128)(2,1)}, u32[]{:S(2)}, u32[]{:S(2)}) collective-permute-start(bf16[4,128,512]{2,1,0:T(8,128)(2,1)} %collective-permute-done.112.refs_11_), channel_id=1, source_target_pairs={{6,7},{7,6},{14,15},{15,14},{22,23},{23,22},{30,31},{31,30}} | collective-permute-start | bytes 1572872 | tf_op jit(solution)/shard_map/ppermute | solution.py:370
  508.7 33.5 %collective-permute-start.53 = (bf16[4,128,512]{2,1,0:T(8,128)(2,1)S(1)}, bf16[4,128,512]{2,1,0:T(8,128)(2,1)S(1)}, u32[]{:S(2)}, u32[]{:S(2)}) collective-permute-start(bf16[4,128,512]{2,1,0:T(8,128)(2,1)S(1)} %broadcast_select_fusion.7), channel_id=1, source_target_pairs={{0,1},{1,0},{2,3},{3,2},{4,5},{5,4},{6,7},{7,6},{8,9},{9,8},{10,11... | collective-permute-start | bytes 1572872 | tf_op jit(solution)/shard_map/ppermute | solution.py:370
  512.2 30.0 %collective-permute-start.58 = (bf16[4,128,512]{2,1,0:T(8,128)(2,1)}, bf16[4,128,512]{2,1,0:T(8,128)(2,1)S(1)}, u32[]{:S(2)}, u32[]{:S(2)}) collective-permute-start(bf16[4,128,512]{2,1,0:T(8,128)(2,1)} %collective-permute-done.55.refs_11_), channel_id=1, source_target_pairs={{6,7},{7,6},{14,15},{15,14},{22,23},{23,22},{30,31},{31,30}} | collective-permute-start | bytes 1572872 | tf_op jit(solution)/shard_map/ppermute | solution.py:370
  (196 other events, 9062.7 us)
